TPU v7x, 256 devices: a whole 4x4x8 slice. The times are simulated.
256 devices in a mesh: front: 4 (over x), row: 16 (over z, core), col: 4 (over y).
Axes of the slice: x: 4, y: 4, z: 8, core: 2. Of those that a mesh axis runs over, the one named last changes fastest.
Arguments:
- front_matrix: float32 [4, 8192, 8192], P('front', 'row', 'col'), may hold values from -1.1 to 24, as said below
- child_update: float32 [4, 4096, 4096], P('front', 'row', 'col'), may hold values from -0.6 to 2, as said below
- block_map: int32 [4, 32], P('front'), may hold values from 0 to 63, as said below
- front_order: int32 [4], P('front'), may hold values from 4096 to 8192, as said below
Outputs:
- panel_factor: float32 [4, 8192, 512], P('front', 'row')
- schur_update: float32 [4, 8192, 8192], P('front', 'row', 'col')
Inputs may be any that keep to these rules, and one draw needn't show every extreme that they name: `block_map`: each front's row names 32 different front blocks. Child block b lands in front run r or (r + 1) mod 16, where r = b // 2 and a front block's run is its index // 4; the last block of every child run lands in the next run. `front_order`: multiples of 128; some front has order 8192. `front_matrix`: each front is symmetric, and the leading 1 * 512 square block of every assembled front is positive definite. `child_update`: each update matrix is symmetric.
All inputs are finite; a program needn't handle non-finite values.
Results may differ from a plain program's by a relative error of at most 0.0003.
Values sent between devices are 32-bit elements; how exact they have to be, the bound alone decides.
No kernel may reach another device: no remote copies, remote signals or barrier semaphores. Data moves between devices by JAX's collectives and lax.ppermute only.
A program may use at most 128 MiB of HBM per device.

v0:
```python
import jax
import jax.numpy as jnp
from jax import lax
from jax.sharding import PartitionSpec as P

BLOCK = 128
PANEL = 512


def from_partner(array, axis, apart):
    return lax.ppermute(array, axis, [(i, i ^ 1 << apart) for i in range(lax.axis_size(axis))])


def shifted(block, axis, distance):
    devices = range(lax.axis_size(axis))
    route = [((i - distance) % len(devices), i) for i in devices]
    return lax.ppermute(block, axis, route)


def broadcast(value, axis, source):
    kept = jnp.where(lax.axis_index(axis) == source, value, 0).astype(value.dtype)
    return lax.psum(kept, axis)


def body(front_matrix, child_update, block_map, front_order):
    row_count = lax.axis_size("row")
    row_index = lax.axis_index("row")
    col_index = lax.axis_index("col")
    local_rows = front_matrix.shape[1]
    local_cols = front_matrix.shape[2]
    row_blocks = local_rows // BLOCK
    col_blocks = local_cols // BLOCK
    child_cols = child_update.shape[2]
    mapping = block_map[0]
    highest = lax.Precision.HIGHEST
    incoming = from_partner(child_update[0], "front", 0)
    run_length = incoming.shape[0] // BLOCK
    arrived = shifted(incoming, "row", 1)
    before = (row_index + row_count - 1) % row_count
    own_ids = row_index * run_length + jnp.arange(run_length)
    prior_ids = before * run_length + jnp.arange(run_length)
    block_ids = jnp.concatenate([own_ids, prior_ids])
    targets = jnp.take(mapping, block_ids)
    valid = targets // row_blocks == row_index
    local_block = targets - row_index * row_blocks
    select = ((local_block[None, :] == jnp.arange(row_blocks)[:, None]) & valid[None, :]).astype(
        jnp.float32
    )
    stacked = jnp.concatenate([incoming, arrived], axis=0).reshape(
        2 * run_length, BLOCK, child_cols
    )
    placed_rows = jnp.einsum("qb,bxc->qxc", select, stacked, precision=highest).reshape(
        local_rows, child_cols
    )
    piece = lax.all_gather(placed_rows, "col", axis=1, tiled=True)
    count = piece.shape[1] // BLOCK
    col_targets = mapping - col_index * col_blocks
    col_select = (col_targets[None, :] == jnp.arange(col_blocks)[:, None]).astype(jnp.float32)
    blocks = piece.reshape(local_rows, count, BLOCK)
    contribution = jnp.einsum("xbw,qb->xqw", blocks, col_select, precision=highest)
    assembled = front_matrix[0] + contribution.reshape(local_rows, local_cols)
    global_rows = row_index * local_rows + jnp.arange(local_rows)
    global_cols = col_index * local_cols + jnp.arange(local_cols)
    order_len = front_order[0]
    live_rows = global_rows < order_len
    live_cols = global_cols < order_len
    current = jnp.where(live_rows[:, None] & live_cols[None, :], assembled, jnp.float32(0.0))
    high = PANEL
    col_root = 0 // local_cols
    col_offset = 0 % local_cols
    row_root = 0 // local_rows
    column_block = broadcast(current[:, col_offset : col_offset + PANEL], "col", col_root)
    diag_block = broadcast(column_block, "row", row_root)
    pivot_all = broadcast(current, "row", row_root)
    lower = jnp.linalg.cholesky(diag_block)
    column_factor = lax.linalg.triangular_solve(lower, pivot_all, left_side=True, lower=True)
    row_factor = lax.linalg.triangular_solve(
        lower, column_block, left_side=False, lower=True, transpose_a=True
    )

    def trailing(state=current, left=row_factor, right=column_factor):
        return state - jnp.dot(left, right, precision=highest)

    updated = trailing()
    keep = (global_rows >= high)[:, None] & (global_cols >= high)[None, :]
    current = jnp.where(keep, updated, jnp.float32(0.0))
    return (row_factor[None], current[None])


def solution(mesh):
    return jax.shard_map(
        body,
        mesh=mesh,
        in_specs=(P("front", "row", "col"), P("front", "row", "col"), P("front", None), P("front")),
        out_specs=(P("front", "row", None), P("front", "row", "col")),
        check_vma=False,
    )
```

profile of v0, /device:TPU:1, one launch (start us, length us, event | category | flops | bytes accessed | tf_op | source)
XLA Modules:
  0.0 527.4 jit_solution(10654531094979524507)
XLA Ops:
  7.2 2.1 collective-permute-start
  9.3 21.9 %collective-permute-done = f32[256,1024]{1,0:T(8,128)S(1)} collective-permute-done((f32[256,1024]{1,0:T(8,128)}, f32[256,1024]{1,0:T(8,128)S(1)}, u32[]{:S(2)}, u32[]{:S(2)}) %collective-permute-start) | collective-permute-done | bytes 1048608 | tf_op jit(solution)/shard_map/ppermute | solution.py:11
  31.2 4.2 collective-permute-start.1
  35.5 1.3 gather_fusion
  36.9 10.2 %collective-permute-done.1 = f32[256,1024]{1,0:T(8,128)S(1)} collective-permute-done((f32[256,1024]{1,0:T(8,128)S(1)}, f32[256,1024]{1,0:T(8,128)S(1)}, u32[]{:S(2)}, u32[]{:S(2)}) %collective-permute-start.1) | collective-permute-done | bytes 1048608 | tf_op jit(solution)/shard_map/ppermute | solution.py:17
  47.3 3.2 fusion.23
  50.6 2.5 copy.22
  53.9 5.3 %copy.20 = f32[1,512,2048]{1,2,0:T(8,128)} copy(f32[1,512,2048]{2,1,0:T(8,128)} %param.4) | data formatting | bytes 8388608 | tf_op args[0]
  59.2 84.2 %all-gather.2.cloned.1.call-done = f32[512,4096]{1,0:T(8,128)} async-done(((f32[512,1024]{1,0:T(8,128)}), f32[512,4096]{1,0:T(8,128)}) %all-gather.2.cloned.1.call-update) | async-done | bytes 8388624 | tf_op jit(solution)/shard_map/all_gather | solution.py:55
  143.4 5.2 copy.40
  148.6 4.4 convolution_bitcast_fusion
  153.0 5.3 %copy.23 = f32[512,16,128]{0,2,1:T(8,128)} copy(f32[512,16,128]{2,1,0:T(8,128)} %convolution_bitcast_fusion) | data formatting | bytes 8388608 | tf_op jit(solution)/shard_map/xbw,qb->xqw/transpose | solution.py:60
  158.3 5.2 broadcast_select_fusion
  163.5 1.9 copy-done.1
  165.5 1.1 slice_select_fusion
  166.8 50.4 %all-reduce.5.cloned.1.call-done = f32[512,512]{0,1:T(8,128)} async-done(((f32[512,512]{0,1:T(8,128)}), f32[512,512]{0,1:T(8,128)}) %all-reduce.5.cloned.1.call-update) | async-done | bytes 1048592 | tf_op jit(solution)/shard_map/psum | solution.py:22
  217.2 1.1 broadcast_select_fusion.1
  218.3 128.6 %all-reduce.7.cloned.1.call-done = (f32[512,512]{0,1:T(8,128)}, f32[512,2048]{0,1:T(8,128)}) async-done(((f32[512,512]{0,1:T(8,128)}, f32[512,2048]{0,1:T(8,128)}), (f32[512,512]{0,1:T(8,128)}, f32[512,2048]{0,1:T(8,128)})) %all-reduce.7.cloned.1.call-update) | async-done | bytes 5242896 | tf_op jit(solution)/shard_map/psum | solution.py:22
  347.0 1.6 copy.24
  348.5 1.4 fusion.27
  350.0 11.7 %cholesky.103 = f32[128,128]{1,0:T(8,128)S(1)} custom-call(f32[128,128]{1,0:T(8,128)S(1)} %cholesky.263), custom_call_target="Cholesky" | custom-call | tf_op jit(solution)/shard_map/jit(cholesky)/cholesky | solution.py:75
  361.8 9.8 %custom-call.32 = f32[1,128,128]{1,2,0:T(8,128)S(1)} custom-call(f32[1,128,128]{2,1,0:T(8,128)S(1)} %get-tuple-element.43), custom_call_target="InvertDiagBlocksLowerTriangular" | custom-call | tf_op jit(solution)/shard_map/jit(cholesky)/cholesky | solution.py:75
  371.6 0.3 fusion.41
  371.9 0.3 convolution_subtract_fusion.5
  372.3 11.7 %cholesky.215 = f32[128,128]{1,0:T(8,128)S(1)} custom-call(f32[128,128]{1,0:T(8,128)S(1)} %cholesky.267), custom_call_target="Cholesky" | custom-call | tf_op jit(solution)/shard_map/jit(cholesky)/cholesky | solution.py:75
  384.3 10.2 %custom-call.33 = f32[1,128,128]{1,2,0:T(8,128)S(1)} custom-call(f32[1,128,128]{2,1,0:T(8,128)S(1)} %get-tuple-element.41), custom_call_target="InvertDiagBlocksLowerTriangular" | custom-call | tf_op jit(solution)/shard_map/jit(cholesky)/cholesky | solution.py:75
  394.7 0.3 convolution_dynamic-update-slice_fusion
  395.1 0.6 convolution_subtract_fusion.6
  395.7 11.7 %cholesky.236 = f32[128,128]{1,0:T(8,128)S(1)} custom-call(f32[128,128]{1,0:T(8,128)S(1)} %cholesky.272), custom_call_target="Cholesky" | custom-call | tf_op jit(solution)/shard_map/jit(cholesky)/cholesky | solution.py:75
  407.5 9.8 %custom-call.34 = f32[1,128,128]{1,2,0:T(8,128)S(1)} custom-call(f32[1,128,128]{2,1,0:T(8,128)S(1)} %get-tuple-element.39), custom_call_target="InvertDiagBlocksLowerTriangular" | custom-call | tf_op jit(solution)/shard_map/jit(cholesky)/cholesky | solution.py:75
  417.3 0.3 convolution_dynamic-update-slice_fusion.1
  417.6 0.5 convolution_subtract_fusion.7
  418.1 11.9 %cholesky.253 = f32[128,128]{1,0:T(8,128)S(1)} custom-call(f32[128,128]{1,0:T(8,128)S(1)} %convolution_subtract_fusion.7), custom_call_target="Cholesky" | custom-call | tf_op jit(solution)/shard_map/jit(cholesky)/cholesky | solution.py:75
  430.1 0.6 compare_reduce_fusion.2
  430.8 0.6 compare_reduce_fusion.3
  431.4 0.7 compare_reduce_fusion.1
  432.1 0.7 compare_reduce_fusion
  435.6 8.5 %while.1 = (s32[]{:T(128)}, f32[512,512]{0,1:T(8,128)S(1)}, s32[4,2]{0,1:T(2,128)S(1)}, f32[4,128,128]{2,1,0:T(8,128)S(1)}, s32[]{:T(128)}) while((s32[]{:T(128)}, f32[512,512]{0,1:T(8,128)S(1)}, s32[4,2]{0,1:T(2,128)S(1)}, f32[4,128,128]{2,1,0:T(8,128)S(1)}, s32[]{:T(128)}) %tuple.34), condition=%wide.while_cond, body=%wide.while_body.sunk | while | flops 2 | bytes 393321 | solution.py:77
  435.6 0.5 fusion.96
  436.2 1.4 dynamic-slice.7
  437.8 0.5 fusion.96
  438.3 1.4 dynamic-slice.7
  439.9 0.5 fusion.96
  440.4 1.4 dynamic-slice.7
  442.0 0.5 fusion.96
  442.5 1.4 dynamic-slice.7
  444.0 39.3 %custom-call.35 = f32[4,128,128]{1,2,0:T(8,128)S(1)} custom-call(f32[4,128,128]{2,1,0:T(8,128)S(1)} %get-tuple-element.9), custom_call_target="InvertDiagBlocksLowerTriangular" | custom-call | tf_op jit(solution)/shard_map/triangular_solve | solution.py:77
  483.4 2.4 fusion.25
  485.8 3.0 convolution_subtract_fusion.1
  488.8 1.1 fusion.54
  489.9 3.5 convolution_subtract_fusion
  493.5 1.1 fusion.56
  494.6 5.5 %fusion.17 = f32[128,2048]{0,1:T(8,128)S(1)} fusion(f32[128,2048]{1,0:T(8,128)S(1)} %fusion.56, f32[128,2048]{1,0:T(8,128)S(1)} %fusion.54, f32[128,2048]{1,0:T(8,128)S(1)} %fusion.25, f32[512,2048]{0,1:T(8,128)S(1)} %copy-done.4, f32[512,512]{0,1:T(8,128)S(1)} %get-tuple-element.103), kind=kOutput, calls=%fused_computation.20 | convolution fusion | flops 1209794560 | bytes 5439488 | tf_op jit(solution)/shard_map/triangular_solve | solution.py:76
  500.1 1.1 fusion.58
  501.2 0.4 fusion.38
  501.6 0.4 convolution_subtract_fusion.3
  502.0 0.4 fusion.55
  502.5 0.5 convolution_subtract_fusion.2
  502.9 0.4 fusion.57
  503.4 0.7 convolution_subtract_fusion.4
  504.1 0.4 fusion.59
  504.6 9.2 %select_bitcast_fusion = f32[1,512,2048]{1,2,0:T(8,128)} fusion(f32[512,2048]{0,1:T(8,128)S(1)} %copy-done.2, f32[128,2048]{1,0:T(8,128)S(1)} %fusion.58, f32[128,2048]{1,0:T(8,128)S(1)} %fusion.56, f32[128,2048]{1,0:T(8,128)S(1)} %fusion.54, f32[128,2048]{1,0:T(8,128)S(1)} %fusion.25, pred[512]{0:T(512)(128)(4,1)S(1)} %fusion.67, ...), kind=kOutput, calls=%fused_computation.13 | convolution fusion | flops 6449528832 | bytes 13634048 | tf_op jit(solution)/shard_map/dot_general | solution.py:82
  513.8 5.3 %copy.35 = f32[1,512,2048]{2,1,0:T(8,128)} copy(f32[1,512,2048]{1,2,0:T(8,128)} %select_bitcast_fusion) | data formatting | bytes 8388608
  519.2 1.3 copy.34
  (61 shorter events, 2.5 us)
Async XLA Ops:
  7.2 136.3 %all-gather.2.cloned.1.call-start = ((), (), s32[]{:S(2)}) async-start(), calls=%async_computation | async-start | bytes 10485760 | tf_op jit(solution)/shard_map/all_gather | solution.py:55
  7.2 24.0 %collective-permute-start = (f32[256,1024]{1,0:T(8,128)}, f32[256,1024]{1,0:T(8,128)S(1)}, u32[]{:S(2)}, u32[]{:S(2)}) collective-permute-start(f32[256,1024]{1,0:T(8,128)} %bitcast.97), channel_id=1, source_target_pairs={{0,64},{64,0},{128,192},{192,128},{1,65},{65,1},{129,193},{193,129... | collective-permute-start | bytes 3145736 | tf_op jit(solution)/shard_map/ppermute | solution.py:11
  31.2 16.0 %collective-permute-start.1 = (f32[256,1024]{1,0:T(8,128)S(1)}, f32[256,1024]{1,0:T(8,128)S(1)}, u32[]{:S(2)}, u32[]{:S(2)}) collective-permute-start(f32[256,1024]{1,0:T(8,128)S(1)} %collective-permute-done), channel_id=1, source_target_pairs={{60,0},{0,4},{4,8},{8,12},{12,16},{16,20},{20,24},{24,28},{28,32},... | collective-permute-start | bytes 3145736 | tf_op jit(solution)/shard_map/ppermute | solution.py:17
  53.1 164.1 %all-reduce.5.cloned.1.call-start = ((), (), s32[]{:S(2)}) async-start(), calls=%async_computation.1 | async-start | bytes 2097152 | tf_op jit(solution)/shard_map/psum | solution.py:22
  53.8 5.4 %copy-start = (s32[1,32]{1,0:T(1,128)S(1)}, s32[1,32]{1,0:T(1,128)}, u32[]{:S(2)}) copy-start(s32[1,32]{1,0:T(1,128)} %param.6) | copy-start | bytes 388
  163.5 1.9 copy-start.1
  166.6 180.4 %all-reduce.7.cloned.1.call-start = ((), (), s32[]{:S(2)}) async-start(), calls=%async_computation.2 | async-start | bytes 10485760 | tf_op jit(solution)/shard_map/psum | solution.py:22
  483.4 6.6 %copy-start.4 = (f32[512,2048]{0,1:T(8,128)S(1)}, f32[512,2048]{0,1:T(8,128)}, u32[]{:S(2)}) copy-start(f32[512,2048]{0,1:T(8,128)} %get-tuple-element.31) | copy-start | bytes 12582916
  494.6 6.6 %copy-start.3 = (f32[512,512]{0,1:T(8,128)S(1)}, f32[512,512]{0,1:T(8,128)}, u32[]{:S(2)}) copy-start(f32[512,512]{0,1:T(8,128)} %all-reduce.5.cloned.1.call-done) | copy-start | bytes 3145732
  501.2 3.4 copy-start.2
Sparse Core Ops, SparseCore 0:
  53.3 90.1 all-gather.1
  166.7 50.4 all-reduce.4
  220.4 126.5 all-reduce.6
where the time goes:
time: 536 us; the launch traced here: 527 us
  waiting for transfers between devices  295 us (55%)
  other arithmetic  128 us (24%)
  matrix products  40.2 us (8%)
  local copies, waits for them, and re-layouts  38.8 us (7%)
  between operations  17.8 us (3%)
  starting transfers between devices  6.7 us (1%)
    psum x2, waiting for transfers between devices, broadcast(): return lax.psum(kept, axis)  179 us
    all_gather x1, waiting for transfers between devices, body(): piece = lax.all_gather(placed_rows, 'col', axis=1, tiled=True)  84.2 us
    another operation x15, other arithmetic, body(): lower = jnp.linalg.cholesky(diag_block)  79.6 us
    another operation x3, other arithmetic, body(): lax.linalg.triangular_solve(lower, column_block, left_side=False, lower=T...  39.4 us
    ppermute x1, waiting for transfers between devices, from_partner(): lax.ppermute(array, axis, [(i, i ^ 1 << apart) for i in range(lax.axis_si...  21.9 us
    unnamed x14, local copies, waits for them, and re-layouts  19.1 us
    another operation x7, matrix products, body(): lax.linalg.triangular_solve(lower, pivot_all, left_side=True, lower=True)  17.8 us
  transfers between devices with their start and end apart: 5, of which 5 were waited for; matrix products, arithmetic and copies ran while one was open for 1% of the time, Pallas kernels for 0%

commit v1 on v0

v1 whole, which is shorter than its diff:
```python
import jax
import jax.numpy as jnp
from jax import lax
from jax.experimental import pallas as pl
from jax.experimental.pallas import tpu as pltpu
from jax.sharding import PartitionSpec as P

BLOCK = 128
PANEL = 512
FRONTS, ROWS, COLS = 4, 16, 4
AXES = ("front", "row", "col")
HIGHEST = lax.Precision.HIGHEST
MIB = 2**20


def permute(x, route):
    def flat(f, r, c):
        return (f * ROWS + r) * COLS + c

    pairs = []
    for f in range(FRONTS):
        for r in range(ROWS):
            for c in range(COLS):
                target = route(f, r, c)
                if target is not None:
                    pairs.append((flat(f, r, c), flat(*target)))
    return lax.ppermute(x, AXES, pairs)


def dot(a, b, ca, cb):
    return lax.dot_general(
        a, b, (((ca,), (cb,)), ((), ())), precision=HIGHEST, preferred_element_type=jnp.float32
    )


def vmem():
    return pl.BlockSpec(memory_space=pltpu.VMEM)


def smem():
    return pl.BlockSpec(memory_space=pltpu.SMEM)


def place(dst, col_off, bmap, run, rows, cols, tile):
    for row_id, row_part in rows:
        t = bmap[0, row_id]
        for col_id, fetch in cols:
            u = bmap[0, col_id]

            @pl.when((t // 4 == run) & (u // 4 == tile))
            def _():
                at_r = pl.ds(pl.multiple_of((t % 4) * BLOCK, BLOCK), BLOCK)
                at_c = pl.ds(pl.multiple_of(col_off + (u % 4) * BLOCK, BLOCK), BLOCK)
                dst[at_r, at_c] = dst[at_r, at_c] + fetch(row_part)


def panel_kernel(bmap, order, front, ea, eb, ed, ee, out, packed):
    r = lax.axis_index("row")
    out[...] = front[...]

    def left(part):
        return ea[...] if part == 0 else eb[(part - 1) * BLOCK : part * BLOCK, :]

    def right(which):
        at = slice(which * BLOCK, (which + 1) * BLOCK)

        def fetch(part):
            return ed[:, at] if part == 0 else ee[(part - 1) * BLOCK : part * BLOCK, at]

        return fetch

    rows = [(2 * r, 0), ((2 * r + 30) % 32, 1), ((2 * r + 31) % 32, 2)]
    cols = [(0, left), (30, right(0)), (31, right(1))]
    place(out, 0, bmap, r, rows, cols, 0)
    index = r * 512 + lax.broadcasted_iota(jnp.int32, out.shape, 0)
    out[...] = jnp.where(index < order[0], out[...], 0.0)
    spot = 0
    for i in range(4):
        for j in range(i + 1):
            packed[spot : spot + BLOCK, :] = out[
                i * BLOCK : (i + 1) * BLOCK, j * BLOCK : (j + 1) * BLOCK
            ]
            spot += BLOCK


def panel_call(bmap, order, front, *pieces):
    return pl.pallas_call(
        panel_kernel,
        grid=(1,),
        in_specs=[smem(), smem(), pl.BlockSpec((512, 512), lambda i: (0, 0))] + [vmem()] * 4,
        out_specs=[vmem(), vmem()],
        out_shape=[
            jax.ShapeDtypeStruct((512, 512), jnp.float32),
            jax.ShapeDtypeStruct((1280, 128), jnp.float32),
        ],
        compiler_params=pltpu.CompilerParams(vmem_limit_bytes=16 * MIB),
        name="panel",
    )(bmap, order, front, *pieces)


def reciprocal(d):
    r = pl.reciprocal(d, approx=True)
    r = r * (2.0 - d * r)
    return r * (2.0 - d * r)


def sweep(groups):
    lane = lax.broadcasted_iota(jnp.int32, (8, 128), 1)
    sub = lax.broadcasted_iota(jnp.int32, (8, 128), 0)
    w = list(groups)

    def across(v, k):
        return jnp.broadcast_to(v[:, k : k + 1], (8, 128))

    def down(v, k):
        return jnp.broadcast_to(v[k : k + 1, :], (8, 128))

    for g in range(16):
        base = 8 * g
        top = w[g]
        col = [across(top, base + j) for j in range(8)]
        inverse, pivot = [], {}
        for j in range(8):
            inverse.append(reciprocal(down(col[j], j)))
            m = jnp.where(sub > j, col[j] * inverse[j], 0.0)
            row = jnp.where(lane == base + j, 1.0, down(top, j))
            top = jnp.where((lane == base + j) & (sub > j), 0.0, top) - m * row
            for q in range(j + 1, 8):
                pivot[j, q] = down(col[q], j)
                col[q] = col[q] - m * pivot[j, q]
        w[g] = top
        inside = (lane >= base) & (lane < base + 8)
        rows = []
        for j in range(8):
            later = (lane > base + j) & (lane < base + 8)
            rows.append(jnp.where(lane == base + j, 1.0, jnp.where(later, 0.0, down(top, j))))
        for h in range(g + 1, 16):
            c = [across(w[h], base + j) for j in range(8)]
            acc = jnp.where(inside, 0.0, w[h])
            for j in range(8):
                m = c[j] * inverse[j]
                for q in range(j + 1, 8):
                    c[q] = c[q] - m * pivot[j, q]
                acc = acc - m * rows[j]
            w[h] = acc
    return w


def factor_kernel(p0, p1, p2, p3, out, packed, work, low):
    c = lax.axis_index("col")
    part = p0.shape[0]
    for s, p in enumerate((p0, p1, p2, p3)):
        packed[pl.ds(pl.multiple_of(((c + 4 - s) % 4) * part, part), part), :] = p[...]
    spot = 0
    for i in range(4):
        for j in range(i + 1):
            work[i * BLOCK : (i + 1) * BLOCK, j * BLOCK : (j + 1) * BLOCK] = packed[
                spot : spot + BLOCK, :
            ]
            spot += BLOCK
    out[...] = jnp.zeros_like(out)
    ri = lax.broadcasted_iota(jnp.int32, (BLOCK, BLOCK), 0)
    ci = lax.broadcasted_iota(jnp.int32, (BLOCK, BLOCK), 1)

    def step(j, carry):
        off = pl.multiple_of(j * BLOCK, BLOCK)
        groups = [
            work[pl.ds(pl.multiple_of(off + 8 * g, 8), 8), pl.ds(off, BLOCK)] for g in range(16)
        ]
        w = jnp.concatenate(sweep(groups), axis=0)
        scale = lax.rsqrt(jnp.sum(jnp.where(ri == ci, w, 0.0), axis=1, keepdims=True))
        inv = jnp.where(ri > ci, w, jnp.where(ri == ci, 1.0, 0.0)) * scale
        out[pl.ds(off, BLOCK), pl.ds(off, BLOCK)] = inv
        for jj in range(4):
            lo, hi = jj * BLOCK, (jj + 1) * BLOCK

            @pl.when(j == jj)
            def _():
                if jj < 3:
                    below = dot(work[hi:, lo:hi], inv, 1, 1)
                    work[hi:, hi:] = work[hi:, hi:] - dot(below, below, 1, 1)
                    low[hi:, lo:hi] = below
                if jj > 0:
                    out[lo:hi, :lo] = -dot(inv, dot(low[lo:hi, :lo], out[:lo, :lo], 1, 0), 1, 0)

        return carry

    lax.fori_loop(0, 4, step, 0)


def factor_call(*pieces):
    return pl.pallas_call(
        factor_kernel,
        in_specs=[vmem()] * 4,
        out_specs=vmem(),
        out_shape=jax.ShapeDtypeStruct((512, 512), jnp.float32),
        scratch_shapes=[
            pltpu.VMEM((1280, 128), jnp.float32),
            pltpu.VMEM((512, 512), jnp.float32),
            pltpu.VMEM((512, 512), jnp.float32),
        ],
        compiler_params=pltpu.CompilerParams(vmem_limit_bytes=16 * MIB),
        name="factor",
    )(*pieces)


def update_kernel(
    bmap, order, front, own, prev, edge, a0, a1, a2, a3, linv, a_col, x_out, s_out, a_row, z
):
    r = lax.axis_index("row")
    c = lax.axis_index("col")
    j = pl.program_id(0)

    @pl.when(j == 0)
    def _():
        for s, p in enumerate((a0, a1, a2, a3)):
            at = pl.ds(pl.multiple_of(((c + 4 - s) % 4) * BLOCK, BLOCK), BLOCK)
            a_row[at, :] = p[...]
        x = dot(a_row[...], linv[...], 1, 1)
        x_out[...] = x
        z[...] = dot(x, linv[...], 1, 0)

    s_out[...] = front[...]
    rows = [(2 * r, 0), ((2 * r + 30) % 32, 1), ((2 * r + 31) % 32, 2)]

    def main(k):
        at = slice(k * BLOCK, (k + 1) * BLOCK)

        def fetch(part):
            return own[:BLOCK, at] if part == 0 else prev[(part - 1) * BLOCK : part * BLOCK, at]

        return fetch

    def side(k):
        at = slice(k * BLOCK, (k + 1) * BLOCK)
        return lambda part: edge[part * BLOCK : (part + 1) * BLOCK, at]

    for t in range(4):

        @pl.when(j == t)
        def _():
            first = (8 * c + 2 * t + 30) % 32
            second = (8 * c + 2 * t + 31) % 32
            if t == 0:
                cols = [(first, side(0)), (second, side(1))]
            else:
                cols = [(first, main(2 * t - 2)), (second, main(2 * t - 1))]
            cols.append((8 * c + 2 * t, main(2 * t)))
            place(s_out, 0, bmap, r, rows, cols, 4 * c + t)

    row = r * 512 + lax.broadcasted_iota(jnp.int32, (512, 1), 0)
    col = (4 * c + j) * 512 + lax.broadcasted_iota(jnp.int32, (1, 512), 1)
    keep = (row >= PANEL) & (row < order[0]) & (col >= PANEL) & (col < order[0])
    s_out[...] = jnp.where(keep, s_out[...] - dot(z[...], a_col[...], 1, 1), 0.0)


def update_call(bmap, order, front, own, prev, edge, a_parts, linv, a_col):
    return pl.pallas_call(
        update_kernel,
        grid=(4,),
        in_specs=[smem(), smem(), pl.BlockSpec((512, 512), lambda j: (0, j))]
        + [vmem()] * 8
        + [pl.BlockSpec((512, 512), lambda j: (j, 0))],
        out_specs=[
            pl.BlockSpec((512, 512), lambda j: (0, 0)),
            pl.BlockSpec((512, 512), lambda j: (0, j)),
        ],
        out_shape=[
            jax.ShapeDtypeStruct((512, 512), jnp.float32),
            jax.ShapeDtypeStruct((512, 2048), jnp.float32),
        ],
        scratch_shapes=[
            pltpu.VMEM((512, 512), jnp.float32),
            pltpu.VMEM((512, 512), jnp.float32),
        ],
        compiler_params=pltpu.CompilerParams(vmem_limit_bytes=40 * MIB),
        name="update",
    )(bmap, order, front, own, prev, edge, *a_parts, linv, a_col)


def total(first, *rest):
    for x in rest:
        first = first + x
    return first


def body(front_matrix, child_update, bmap, order):
    front = front_matrix[0]
    child = child_update[0]
    c = lax.axis_index("col")

    ea = permute(child[:128, :128], lambda f, r, c: (f ^ 1, r, 0) if c == 0 else None)
    eb = permute(child[:, :128], lambda f, r, c: (f ^ 1, (r + 1) % ROWS, 0) if c == 0 else None)
    ed = permute(child[:128, 768:], lambda f, r, c: (f ^ 1, r, 0) if c == 3 else None)
    ee = permute(child[:, 768:], lambda f, r, c: (f ^ 1, (r + 1) % ROWS, 0) if c == 3 else None)
    panel, packed = panel_call(bmap, order, front, ea, eb, ed, ee)

    def share(x, rows):
        parts = [x[q * rows : (q + 1) * rows] for q in range(4)]
        return parts

    quarter = share(packed, 320)
    got = [
        permute(quarter[q], lambda f, r, c, q=q: (f, 0, q) if r == 0 and c == 0 else None)
        for q in (1, 2, 3)
    ]
    d = jnp.where(c == 0, quarter[0], total(*got))
    d1 = permute(d, lambda f, r, c: (f, 6, c) if r == 0 else None)
    d2 = permute(d, lambda f, r, c: (f, 12, c) if r == 0 else None)
    here = lax.axis_index("row") == 0
    d = jnp.where(here, d, d1 + d2)
    d1 = permute(d, lambda f, r, c: (f, (r + 2) % ROWS, c) if r in (0, 6, 12) else None)
    d2 = permute(d, lambda f, r, c: (f, r - 2, c) if r in (6, 12) else None)
    row = lax.axis_index("row")
    d = jnp.where((row == 0) | (row == 6) | (row == 12), d, d1 + d2)
    d1 = permute(d, lambda f, r, c: (f, r + 1, c) if r % 2 == 0 else None)
    d = jnp.where(row % 2 == 0, d, d1)

    quarter = share(panel, 128)
    got = [
        permute(quarter[q], lambda f, r, c, q=q: (f, r, q) if c == 0 else None) for q in (1, 2, 3)
    ]
    mine = jnp.where(c == 0, quarter[0], total(*got))
    got = [
        permute(
            quarter[q], lambda f, r, c, q=q: (f, 4 * (r % 4) + q, r // 4) if c == 0 else None
        )
        for q in range(4)
    ]
    a_col = lax.all_gather(total(*got), "row", axis=0, tiled=True)

    d_parts = [d] + [permute(d, lambda f, r, c, s=s: (f, r, (c + s) % COLS)) for s in (1, 2, 3)]
    a_parts = [mine] + [
        permute(mine, lambda f, r, c, s=s: (f, r, (c + s) % COLS)) for s in (1, 2, 3)
    ]

    own = permute(child, lambda f, r, c: (f ^ 1, r, c))
    prev = permute(own, lambda f, r, c: (f, (r + 1) % ROWS, c))
    edge = jnp.concatenate([own[:128, 768:], prev[:, 768:]], axis=0)
    edge = permute(edge, lambda f, r, c: (f, r, (c + 1) % COLS))

    linv = factor_call(*d_parts)
    x, s = update_call(bmap, order, front, own, prev, edge, a_parts, linv, a_col)
    return x[None], s[None]


def solution(mesh):
    return jax.shard_map(
        body,
        mesh=mesh,
        in_specs=(P("front", "row", "col"), P("front", "row", "col"), P("front", None), P("front")),
        out_specs=(P("front", "row", None), P("front", "row", "col")),
        check_vma=False,
    )
```

time: 536 us -> 206 us (0.38); the launches traced: 527 us -> 204 us
  waiting for transfers between devices: 295 us -> 80 us
  other arithmetic: 128 us -> 1.04 us
  starting transfers between devices: 6.7 us -> 50.6 us
  matrix products: 40.2 us -> 0 us
  Pallas kernels: 0 us -> 39.4 us
  local copies, waits for them, and re-layouts: 38.8 us -> 17.7 us
    psum x2 -> x0, waiting for transfers between devices: 179 us -> none  [broadcast(): return lax.psum(kept, axis)]
    another operation x18 -> x0, other arithmetic: 119 us -> none  [the longest x15 79.6 us: body(): lower = jnp.linalg.cholesky(diag_block)]
    all_gather x1, waiting for transfers between devices: 84.2 us -> 0.01 us  [body(): a_col = lax.all_gather(total(*got), 'row', axis=0, tiled=True)]
    ppermute x2 -> x28, waiting for transfers between devices: 32.1 us -> 80 us  [permute(): return lax.ppermute(x, AXES, pairs)]
    ppermute x2 -> x28, starting transfers between devices: 6.37 us -> 50.6 us  [permute(): return lax.ppermute(x, AXES, pairs)]
    pallas_call x0 -> x3, Pallas kernels: none -> 39.4 us  [the longest x1 24.4 us: factor_call(): pl.pallas_call(factor_kernel, in_specs=[vmem()] * 4, out_specs=vmem(), ou...]
    another operation x20 -> x0, matrix products: 23.3 us -> none  [the longest x7 17.8 us: body(): lax.linalg.triangular_solve(lower, pivot_all, left_side=True, lower=True)]
    dot_general x3 -> x0, matrix products: 16.9 us -> none  [the longest x1 9.23 us: trailing(): return state - jnp.dot(left, right, precision=highest)]
  transfers between devices with their start and end apart: 5 -> 29, of which waited for: 5 -> 10; matrix products, arithmetic and copies ran while one was open for 1% -> 1% of each run, Pallas kernels for 0% -> 12%
where the time goes in v1:
time: 206 us; the launch traced here: 204 us
  waiting for transfers between devices  80 us (39%)
  starting transfers between devices  50.6 us (25%)
  Pallas kernels  39.4 us (19%)
  local copies, waits for them, and re-layouts  17.7 us (9%)
  between operations  15.1 us (7%)
    ppermute x28, waiting for transfers between devices, permute(): return lax.ppermute(x, AXES, pairs)  80 us
    ppermute x28, starting transfers between devices, permute(): return lax.ppermute(x, AXES, pairs)  50.6 us
    pallas_call x1, Pallas kernels, factor_call(): pl.pallas_call(factor_kernel, in_specs=[vmem()] * 4, out_specs=vmem(), ou...  24.4 us
    pallas_call x1, Pallas kernels, update_call(): pl.pallas_call(update_kernel, grid=(4,), in_specs=[smem(), smem(), pl.Blo...  14.1 us
    unnamed x26, local copies, waits for them, and re-layouts  13.9 us
  transfers between devices with their start and end apart: 29, of which 10 were waited for; matrix products, arithmetic and copies ran while one was open for 1% of the time, Pallas kernels for 12%

profile of v1, /device:TPU:1, one launch (start us, length us, event | category | flops | bytes accessed | tf_op | source)
XLA Modules:
  0.0 203.9 jit_solution(15499652589956754665)
XLA Ops:
  7.2 0.0 all-gather.2.cloned.1.call-start
  7.2 1.0 slice.61
  8.2 1.3 collective-permute-start.6
  9.5 0.9 slice.59
  10.4 5.9 %collective-permute-start.4 = (f32[256,128]{1,0:T(8,128)S(1)}, f32[256,128]{1,0:T(8,128)S(1)}, u32[]{:S(2)}, u32[]{:S(2)}) collective-permute-start(f32[256,128]{1,0:T(8,128)S(1)} %slice.59), channel_id=1, source_target_pairs={{0,68},{4,72},{8,76},{12,80},{16,84},{20,88},{24,92},{28,96},{32,1... | collective-permute-start | bytes 393224 | tf_op jit(solution)/shard_map/ppermute | solution.py:27
  16.3 0.9 slice.60
  17.2 1.3 collective-permute-start.5
  18.5 0.8 slice.58
  19.3 2.2 %collective-permute-start.3 = (f32[128,128]{1,0:T(8,128)S(1)}, f32[128,128]{1,0:T(8,128)S(1)}, u32[]{:S(2)}, u32[]{:S(2)}) collective-permute-start(f32[128,128]{1,0:T(8,128)S(1)} %slice.58), channel_id=1, source_target_pairs={{0,64},{4,68},{8,72},{12,76},{16,80},{20,84},{24,88},{28,92},{32,9... | collective-permute-start | bytes 196616 | tf_op jit(solution)/shard_map/ppermute | solution.py:27
  22.1 2.9 %collective-permute-done.3.ea = f32[128,128]{1,0:T(8,128)S(1)} collective-permute-done((f32[128,128]{1,0:T(8,128)S(1)}, f32[128,128]{1,0:T(8,128)S(1)}, u32[]{:S(2)}, u32[]{:S(2)}) %collective-permute-start.3) | collective-permute-done | bytes 65568 | tf_op jit(solution)/shard_map/ppermute | solution.py:27
  25.1 0.0 collective-permute-done.4.eb
  25.1 1.1 collective-permute-done.5.ed
  26.2 0.0 collective-permute-done.6.ee
  26.2 2.2 %copy-done = f32[1,512,2048]{2,1,0:T(8,128)S(1)} copy-done((f32[1,512,2048]{2,1,0:T(8,128)S(1)}, f32[1,512,2048]{2,1,0:T(8,128)}, u32[]{:S(2)}) %copy-start) | copy-done | bytes 4194328
  28.4 0.7 copy-done.11
  29.1 0.9 panel.1
  30.0 0.1 fusion.1
  30.1 1.3 collective-permute-start.8
  31.4 1.3 collective-permute-start.9
  32.7 1.3 collective-permute-start.7
  34.0 4.6 %collective-permute-start.26 = (f32[128,512]{1,0:T(8,128)S(1)}, f32[128,512]{1,0:T(8,128)S(1)}, u32[]{:S(2)}, u32[]{:S(2)}) collective-permute-start(f32[128,512]{1,0:T(8,128)S(1)} %get-tuple-element.12), channel_id=1, source_target_pairs={{0,8},{4,24},{8,40},{12,56},{16,9},{20,25},{24,41},{28,57},{32,10}... | collective-permute-start | bytes 786440 | tf_op jit(solution)/shard_map/ppermute | solution.py:27
  38.6 3.0 %collective-permute-start.27 = (f32[128,512]{1,0:T(8,128)S(1)}, f32[128,512]{1,0:T(8,128)S(1)}, u32[]{:S(2)}, u32[]{:S(2)}) collective-permute-start(f32[128,512]{1,0:T(8,128)S(1)} %get-tuple-element.13), channel_id=1, source_target_pairs={{0,12},{4,28},{8,44},{12,60},{16,13},{20,29},{24,45},{28,61},{32,1... | collective-permute-start | bytes 786440 | tf_op jit(solution)/shard_map/ppermute | solution.py:27
  41.6 1.9 collective-permute-start.25
  43.6 0.1 fusion
  43.7 0.0 copy-start.12
  43.7 3.4 %collective-permute-start.24 = (f32[128,512]{1,0:T(8,128)S(1)}, f32[128,512]{1,0:T(8,128)S(1)}, u32[]{:S(2)}, u32[]{:S(2)}) collective-permute-start(f32[128,512]{1,0:T(8,128)S(1)} %get-tuple-element.10), channel_id=1, source_target_pairs={{0,0},{4,16},{8,32},{12,48},{16,1},{20,17},{24,33},{28,49},{32,2},... | collective-permute-start | bytes 786440 | tf_op jit(solution)/shard_map/ppermute | solution.py:27
  47.1 4.5 %collective-permute-done.27 = f32[128,512]{1,0:T(8,128)S(1)} collective-permute-done((f32[128,512]{1,0:T(8,128)S(1)}, f32[128,512]{1,0:T(8,128)S(1)}, u32[]{:S(2)}, u32[]{:S(2)}) %collective-permute-start.27) | collective-permute-done | bytes 262176 | tf_op jit(solution)/shard_map/ppermute | solution.py:27
  51.7 7.0 %collective-permute-done.25 = f32[128,512]{1,0:T(8,128)S(1)} collective-permute-done((f32[128,512]{1,0:T(8,128)S(1)}, f32[128,512]{1,0:T(8,128)S(1)}, u32[]{:S(2)}, u32[]{:S(2)}) %collective-permute-start.25) | collective-permute-done | bytes 262176 | tf_op jit(solution)/shard_map/ppermute | solution.py:27
  58.7 6.7 %collective-permute-done.24 = f32[128,512]{1,0:T(8,128)S(1)} collective-permute-done((f32[128,512]{1,0:T(8,128)S(1)}, f32[128,512]{1,0:T(8,128)S(1)}, u32[]{:S(2)}, u32[]{:S(2)}) %collective-permute-start.24) | collective-permute-done | bytes 262176 | tf_op jit(solution)/shard_map/ppermute | solution.py:27
  65.4 0.8 add_add_fusion
  66.2 0.0 all-gather.2.cloned.1.call-update
  66.2 0.4 collective-permute-start
  66.6 0.7 collective-permute-start.14
  67.3 0.7 collective-permute-start.15
  68.0 0.7 collective-permute-start.13
  68.8 0.7 collective-permute-start.17
  69.4 0.7 collective-permute-start.16
  70.1 10.1 %collective-permute-done.own = f32[256,1024]{1,0:T(8,128)S(1)} collective-permute-done((f32[256,1024]{1,0:T(8,128)}, f32[256,1024]{1,0:T(8,128)S(1)}, u32[]{:S(2)}, u32[]{:S(2)}) %collective-permute-start) | collective-permute-done | bytes 1048608 | tf_op jit(solution)/shard_map/ppermute | solution.py:27
  80.3 7.9 %collective-permute-start.1 = (f32[256,1024]{1,0:T(8,128)S(1)}, f32[256,1024]{1,0:T(8,128)S(1)}, u32[]{:S(2)}, u32[]{:S(2)}) collective-permute-start(f32[256,1024]{1,0:T(8,128)S(1)} %collective-permute-done.own), channel_id=1, source_target_pairs={{0,4},{1,5},{2,6},{3,7},{4,8},{5,9},{6,10},{7,11},{8,12},{9,13},{1... | collective-permute-start | bytes 3145736 | tf_op jit(solution)/shard_map/ppermute | solution.py:27
  88.2 0.7 collective-permute-start.19
  88.9 0.7 collective-permute-start.18
  89.7 1.3 collective-permute-start.20
  91.0 15.0 %collective-permute-done.20 = f32[320,128]{1,0:T(8,128)S(1)} collective-permute-done((f32[320,128]{1,0:T(8,128)S(1)}, f32[320,128]{1,0:T(8,128)S(1)}, u32[]{:S(2)}, u32[]{:S(2)}) %collective-permute-start.20) | collective-permute-done | bytes 163872 | tf_op jit(solution)/shard_map/ppermute | solution.py:27
  106.0 2.8 %collective-permute-start.23 = (f32[320,128]{1,0:T(8,128)S(1)}, f32[320,128]{1,0:T(8,128)S(1)}, u32[]{:S(2)}, u32[]{:S(2)}) collective-permute-start(f32[320,128]{1,0:T(8,128)S(1)} %broadcast_select_fusion.p0), channel_id=1, source_target_pairs={{0,3},{1,0},{2,1},{3,2},{4,7},{5,4},{6,5},{7,6},{8,11},{9,8},{10,9... | collective-permute-start | bytes 491528 | tf_op jit(solution)/shard_map/ppermute | solution.py:27
  108.8 9.8 %collective-permute-done.1.prev = f32[256,1024]{1,0:T(8,128)S(1)} collective-permute-done((f32[256,1024]{1,0:T(8,128)S(1)}, f32[256,1024]{1,0:T(8,128)S(1)}, u32[]{:S(2)}, u32[]{:S(2)}) %collective-permute-start.1) | collective-permute-done | bytes 1048608 | tf_op jit(solution)/shard_map/ppermute | solution.py:27
  118.6 0.1 collective-permute-start.2
  118.7 4.5 %collective-permute-start.22 = (f32[320,128]{1,0:T(8,128)S(1)}, f32[320,128]{1,0:T(8,128)S(1)}, u32[]{:S(2)}, u32[]{:S(2)}) collective-permute-start(f32[320,128]{1,0:T(8,128)S(1)} %broadcast_select_fusion.p0), channel_id=1, source_target_pairs={{0,2},{1,3},{2,0},{3,1},{4,6},{5,7},{6,4},{7,5},{8,10},{9,11},{10,... | collective-permute-start | bytes 491528 | tf_op jit(solution)/shard_map/ppermute | solution.py:27
  123.2 1.3 collective-permute-start.11
  124.4 0.2 collective-permute-start.10
  124.6 8.6 %collective-permute-done.22.p2 = f32[320,128]{1,0:T(8,128)S(1)} collective-permute-done((f32[320,128]{1,0:T(8,128)S(1)}, f32[320,128]{1,0:T(8,128)S(1)}, u32[]{:S(2)}, u32[]{:S(2)}) %collective-permute-start.22) | collective-permute-done | bytes 163872 | tf_op jit(solution)/shard_map/ppermute | solution.py:27
  133.2 0.0 collective-permute-start.21
  133.2 14.1 %collective-permute-done.21.p1 = f32[320,128]{1,0:T(8,128)S(1)} collective-permute-done((f32[320,128]{1,0:T(8,128)S(1)}, f32[320,128]{1,0:T(8,128)S(1)}, u32[]{:S(2)}, u32[]{:S(2)}) %collective-permute-start.21) | collective-permute-done | bytes 163872 | tf_op jit(solution)/shard_map/ppermute | solution.py:27
  147.4 24.4 %factor.1.linv = f32[512,512]{1,0:T(8,128)S(1)} custom-call(f32[320,128]{1,0:T(8,128)S(1)} %broadcast_select_fusion.p0, f32[320,128]{1,0:T(8,128)S(1)} %collective-permute-done.21.p1, f32[320,128]{1,0:T(8,128)S(1)} %collective-permute-done.22.p2, f32[320,128]{1,0:T(8,128)S(1)} %collective-permute-done.23.p3), custom_call_target="tpu_custom_call" | custom-call | tf_op jit(solution)/shard_map/factor/pallas_call | solution.py:192
  171.8 0.7 copy-done.5
  172.5 0.7 copy-done.7
  173.2 0.7 copy-done.9
  173.9 0.7 copy-done.3
  174.7 2.2 %copy-done.1 = f32[1,512,2048]{2,1,0:T(8,128)S(1)} copy-done((f32[1,512,2048]{2,1,0:T(8,128)S(1)}, f32[1,512,2048]{2,1,0:T(8,128)}, u32[]{:S(2)}) %copy-start.1) | copy-done | bytes 4194328
  176.9 2.2 %copy-done.2 = f32[2048,512]{1,0:T(8,128)S(1)} copy-done((f32[2048,512]{1,0:T(8,128)S(1)}, f32[2048,512]{1,0:T(8,128)}, u32[]{:S(2)}) %copy-start.2) | copy-done | bytes 4194328
  179.0 1.0 copy-done.4
  180.0 0.9 copy-done.6
  181.0 0.9 copy-done.8
  181.9 0.9 copy-done.10
  182.9 14.1 %update.1 = (f32[512,512]{1,0:T(8,128)}, f32[512,2048]{1,0:T(8,128)}) custom-call(s32[1,32]{1,0:T(1,128)S(1)} %copy-done.12, s32[1]{0:T(128)S(6)} %copy.6.order, f32[512,2048]{1,0:T(8,128)S(1)} %bitcast.5, f32[256,1024]{1,0:T(8,128)S(1)} %collective-permute-done.own, f32[256,1024]{1,0:T(8,128)S(1)} %collective-permute-done.1.prev, f32[384,256]{1,0:T(8,128)S(1)} %copy-done.4, ...), custom_call_target="tpu_custom_call" | custom-call | tf_op jit(solution)/shard_map/update/pallas_call | solution.py:258
  (39 shorter events, 0.3 us)
Async XLA Ops:
  7.2 167.5 %all-gather.2.cloned.1.call-start = ((), (), s32[]{:S(2)}) async-start(), calls=%async_computation | async-start | bytes 4456448 | tf_op jit(solution)/shard_map/all_gather | solution.py:330
  8.2 18.0 %collective-permute-start.6 = (f32[256,256]{1,0:T(8,128)S(1)}, f32[256,256]{1,0:T(8,128)S(1)}, u32[]{:S(2)}, u32[]{:S(2)}) collective-permute-start(f32[256,256]{1,0:T(8,128)S(1)} %slice.61), channel_id=1, source_target_pairs={{3,68},{7,72},{11,76},{15,80},{19,84},{23,88},{27,92},{31,96},{35,... | collective-permute-start | bytes 786440 | tf_op jit(solution)/shard_map/ppermute | solution.py:27
  10.4 14.7 %collective-permute-start.4 = (f32[256,128]{1,0:T(8,128)S(1)}, f32[256,128]{1,0:T(8,128)S(1)}, u32[]{:S(2)}, u32[]{:S(2)}) collective-permute-start(f32[256,128]{1,0:T(8,128)S(1)} %slice.59), channel_id=1, source_target_pairs={{0,68},{4,72},{8,76},{12,80},{16,84},{20,88},{24,92},{28,96},{32,1... | collective-permute-start | bytes 393224 | tf_op jit(solution)/shard_map/ppermute | solution.py:27
  17.2 9.0 %collective-permute-start.5 = (f32[128,256]{1,0:T(8,128)S(1)}, f32[128,256]{1,0:T(8,128)S(1)}, u32[]{:S(2)}, u32[]{:S(2)}) collective-permute-start(f32[128,256]{1,0:T(8,128)S(1)} %slice.60), channel_id=1, source_target_pairs={{3,64},{7,68},{11,72},{15,76},{19,80},{23,84},{27,88},{31,92},{35,... | collective-permute-start | bytes 393224 | tf_op jit(solution)/shard_map/ppermute | solution.py:27
  19.3 5.8 %collective-permute-start.3 = (f32[128,128]{1,0:T(8,128)S(1)}, f32[128,128]{1,0:T(8,128)S(1)}, u32[]{:S(2)}, u32[]{:S(2)}) collective-permute-start(f32[128,128]{1,0:T(8,128)S(1)} %slice.58), channel_id=1, source_target_pairs={{0,64},{4,68},{8,72},{12,76},{16,80},{20,84},{24,88},{28,92},{32,9... | collective-permute-start | bytes 196616 | tf_op jit(solution)/shard_map/ppermute | solution.py:27
  26.2 2.2 %copy-start = (f32[1,512,2048]{2,1,0:T(8,128)S(1)}, f32[1,512,2048]{2,1,0:T(8,128)}, u32[]{:S(2)}) copy-start(f32[1,512,2048]{2,1,0:T(8,128)} %param.4) | copy-start | bytes 12582916
  28.4 0.7 copy-start.11
  30.1 11.5 %collective-permute-start.8 = (f32[128,512]{1,0:T(8,128)S(1)}, f32[128,512]{1,0:T(8,128)S(1)}, u32[]{:S(2)}, u32[]{:S(2)}) collective-permute-start(f32[128,512]{1,0:T(8,128)S(1)} %get-tuple-element.12), channel_id=1, source_target_pairs={{0,2},{4,6},{8,10},{12,14},{16,18},{20,22},{24,26},{28,30},{32,34}... | collective-permute-start | bytes 786440 | tf_op jit(solution)/shard_map/ppermute | solution.py:27
  31.4 12.2 %collective-permute-start.9 = (f32[128,512]{1,0:T(8,128)S(1)}, f32[128,512]{1,0:T(8,128)S(1)}, u32[]{:S(2)}, u32[]{:S(2)}) collective-permute-start(f32[128,512]{1,0:T(8,128)S(1)} %get-tuple-element.13), channel_id=1, source_target_pairs={{0,3},{4,7},{8,11},{12,15},{16,19},{20,23},{24,27},{28,31},{32,35}... | collective-permute-start | bytes 786440 | tf_op jit(solution)/shard_map/ppermute | solution.py:27
  32.7 10.9 %collective-permute-start.7 = (f32[128,512]{1,0:T(8,128)S(1)}, f32[128,512]{1,0:T(8,128)S(1)}, u32[]{:S(2)}, u32[]{:S(2)}) collective-permute-start(f32[128,512]{1,0:T(8,128)S(1)} %get-tuple-element.14), channel_id=1, source_target_pairs={{0,1},{4,5},{8,9},{12,13},{16,17},{20,21},{24,25},{28,29},{32,33},... | collective-permute-start | bytes 786440 | tf_op jit(solution)/shard_map/ppermute | solution.py:27
  34.0 13.1 %collective-permute-start.26 = (f32[128,512]{1,0:T(8,128)S(1)}, f32[128,512]{1,0:T(8,128)S(1)}, u32[]{:S(2)}, u32[]{:S(2)}) collective-permute-start(f32[128,512]{1,0:T(8,128)S(1)} %get-tuple-element.12), channel_id=1, source_target_pairs={{0,8},{4,24},{8,40},{12,56},{16,9},{20,25},{24,41},{28,57},{32,10}... | collective-permute-start | bytes 786440 | tf_op jit(solution)/shard_map/ppermute | solution.py:27
  38.6 13.1 %collective-permute-start.27 = (f32[128,512]{1,0:T(8,128)S(1)}, f32[128,512]{1,0:T(8,128)S(1)}, u32[]{:S(2)}, u32[]{:S(2)}) collective-permute-start(f32[128,512]{1,0:T(8,128)S(1)} %get-tuple-element.13), channel_id=1, source_target_pairs={{0,12},{4,28},{8,44},{12,60},{16,13},{20,29},{24,45},{28,61},{32,1... | collective-permute-start | bytes 786440 | tf_op jit(solution)/shard_map/ppermute | solution.py:27
  41.6 17.0 %collective-permute-start.25 = (f32[128,512]{1,0:T(8,128)S(1)}, f32[128,512]{1,0:T(8,128)S(1)}, u32[]{:S(2)}, u32[]{:S(2)}) collective-permute-start(f32[128,512]{1,0:T(8,128)S(1)} %get-tuple-element.14), channel_id=1, source_target_pairs={{0,4},{4,20},{8,36},{12,52},{16,5},{20,21},{24,37},{28,53},{32,6},... | collective-permute-start | bytes 786440 | tf_op jit(solution)/shard_map/ppermute | solution.py:27
  43.7 131.0 %copy-start.12 = (s32[1,32]{1,0:T(1,128)S(1)}, s32[1,32]{1,0:T(1,128)}, u32[]{:S(2)}) copy-start(s32[1,32]{1,0:T(1,128)} %bmap.3) | copy-start | bytes 388
  43.7 21.7 %collective-permute-start.24 = (f32[128,512]{1,0:T(8,128)S(1)}, f32[128,512]{1,0:T(8,128)S(1)}, u32[]{:S(2)}, u32[]{:S(2)}) collective-permute-start(f32[128,512]{1,0:T(8,128)S(1)} %get-tuple-element.10), channel_id=1, source_target_pairs={{0,0},{4,16},{8,32},{12,48},{16,1},{20,17},{24,33},{28,49},{32,2},... | collective-permute-start | bytes 786440 | tf_op jit(solution)/shard_map/ppermute | solution.py:27
  66.2 14.1 %collective-permute-start = (f32[256,1024]{1,0:T(8,128)}, f32[256,1024]{1,0:T(8,128)S(1)}, u32[]{:S(2)}, u32[]{:S(2)}) collective-permute-start(f32[256,1024]{1,0:T(8,128)} %bitcast.1), channel_id=1, source_target_pairs={{0,64},{1,65},{2,66},{3,67},{4,68},{5,69},{6,70},{7,71},{8,72},{9,... | collective-permute-start | bytes 3145736 | tf_op jit(solution)/shard_map/ppermute | solution.py:27
  66.6 2.0 %collective-permute-start.14 = (f32[320,128]{1,0:T(8,128)S(1)}, f32[320,128]{1,0:T(8,128)S(1)}, u32[]{:S(2)}, u32[]{:S(2)}) collective-permute-start(f32[320,128]{1,0:T(8,128)S(1)} %get-tuple-element.15), channel_id=1, source_target_pairs={{0,2},{64,66},{128,130},{192,194}} | collective-permute-start | bytes 491528 | tf_op jit(solution)/shard_map/ppermute | solution.py:27
  67.3 1.4 collective-permute-start.15
  68.0 0.7 collective-permute-start.13
  68.8 19.4 %collective-permute-start.17 = (f32[320,128]{1,0:T(8,128)S(1)}, f32[320,128]{1,0:T(8,128)S(1)}, u32[]{:S(2)}, u32[]{:S(2)}) collective-permute-start(f32[320,128]{1,0:T(8,128)S(1)} %add_select_fusion.3), channel_id=1, source_target_pairs={{0,48},{1,49},{2,50},{3,51},{64,112},{65,113},{66,114},{67,115},{1... | collective-permute-start | bytes 491528 | tf_op jit(solution)/shard_map/ppermute | solution.py:27
  69.4 18.8 %collective-permute-start.16 = (f32[320,128]{1,0:T(8,128)S(1)}, f32[320,128]{1,0:T(8,128)S(1)}, u32[]{:S(2)}, u32[]{:S(2)}) collective-permute-start(f32[320,128]{1,0:T(8,128)S(1)} %add_select_fusion.3), channel_id=1, source_target_pairs={{0,24},{1,25},{2,26},{3,27},{64,88},{65,89},{66,90},{67,91},{128,1... | collective-permute-start | bytes 491528 | tf_op jit(solution)/shard_map/ppermute | solution.py:27
  80.3 38.3 %collective-permute-start.1 = (f32[256,1024]{1,0:T(8,128)S(1)}, f32[256,1024]{1,0:T(8,128)S(1)}, u32[]{:S(2)}, u32[]{:S(2)}) collective-permute-start(f32[256,1024]{1,0:T(8,128)S(1)} %collective-permute-done.own), channel_id=1, source_target_pairs={{0,4},{1,5},{2,6},{3,7},{4,8},{5,9},{6,10},{7,11},{8,12},{9,13},{1... | collective-permute-start | bytes 3145736 | tf_op jit(solution)/shard_map/ppermute | solution.py:27
  88.2 1.4 collective-permute-start.19
  88.9 0.7 collective-permute-start.18
  89.7 16.3 %collective-permute-start.20 = (f32[320,128]{1,0:T(8,128)S(1)}, f32[320,128]{1,0:T(8,128)S(1)}, u32[]{:S(2)}, u32[]{:S(2)}) collective-permute-start(f32[320,128]{1,0:T(8,128)S(1)} %add_select_fusion.1), channel_id=1, source_target_pairs={{0,4},{1,5},{2,6},{3,7},{8,12},{9,13},{10,14},{11,15},{16,20},{17,... | collective-permute-start | bytes 491528 | tf_op jit(solution)/shard_map/ppermute | solution.py:27
  106.0 18.5 %collective-permute-start.23 = (f32[320,128]{1,0:T(8,128)S(1)}, f32[320,128]{1,0:T(8,128)S(1)}, u32[]{:S(2)}, u32[]{:S(2)}) collective-permute-start(f32[320,128]{1,0:T(8,128)S(1)} %broadcast_select_fusion.p0), channel_id=1, source_target_pairs={{0,3},{1,0},{2,1},{3,2},{4,7},{5,4},{6,5},{7,6},{8,11},{9,8},{10,9... | collective-permute-start | bytes 491528 | tf_op jit(solution)/shard_map/ppermute | solution.py:27
  118.6 55.3 %collective-permute-start.2 = (f32[384,256]{1,0:T(8,128)S(1)}, f32[384,256]{1,0:T(8,128)S(1)}, u32[]{:S(2)}, u32[]{:S(2)}) collective-permute-start(f32[384,256]{1,0:T(8,128)S(1)} %pad_maximum_fusion), channel_id=1, source_target_pairs={{0,1},{1,2},{2,3},{3,0},{4,5},{5,6},{6,7},{7,4},{8,9},{9,10},{10,1... | collective-permute-start | bytes 1179656 | tf_op jit(solution)/shard_map/ppermute | solution.py:27
  118.7 14.6 %collective-permute-start.22 = (f32[320,128]{1,0:T(8,128)S(1)}, f32[320,128]{1,0:T(8,128)S(1)}, u32[]{:S(2)}, u32[]{:S(2)}) collective-permute-start(f32[320,128]{1,0:T(8,128)S(1)} %broadcast_select_fusion.p0), channel_id=1, source_target_pairs={{0,2},{1,3},{2,0},{3,1},{4,6},{5,7},{6,4},{7,5},{8,10},{9,11},{10,... | collective-permute-start | bytes 491528 | tf_op jit(solution)/shard_map/ppermute | solution.py:27
  123.2 48.6 %collective-permute-start.12 = (f32[128,512]{1,0:T(8,128)S(1)}, f32[128,512]{1,0:T(8,128)S(1)}, u32[]{:S(2)}, u32[]{:S(2)}) collective-permute-start(f32[128,512]{1,0:T(8,128)S(1)} %get-tuple-element.11.a0), channel_id=1, source_target_pairs={{0,3},{1,0},{2,1},{3,2},{4,7},{5,4},{6,5},{7,6},{8,11},{9,8},{10,9... | collective-permute-start | bytes 786440 | tf_op jit(solution)/shard_map/ppermute | solution.py:27
  123.2 49.3 %collective-permute-start.11 = (f32[128,512]{1,0:T(8,128)S(1)}, f32[128,512]{1,0:T(8,128)S(1)}, u32[]{:S(2)}, u32[]{:S(2)}) collective-permute-start(f32[128,512]{1,0:T(8,128)S(1)} %get-tuple-element.11.a0), channel_id=1, source_target_pairs={{0,2},{1,3},{2,0},{3,1},{4,6},{5,7},{6,4},{7,5},{8,10},{9,11},{10,... | collective-permute-start | bytes 786440 | tf_op jit(solution)/shard_map/ppermute | solution.py:27
  124.4 48.8 %collective-permute-start.10 = (f32[128,512]{1,0:T(8,128)S(1)}, f32[128,512]{1,0:T(8,128)S(1)}, u32[]{:S(2)}, u32[]{:S(2)}) collective-permute-start(f32[128,512]{1,0:T(8,128)S(1)} %get-tuple-element.11.a0), channel_id=1, source_target_pairs={{0,1},{1,2},{2,3},{3,0},{4,5},{5,6},{6,7},{7,4},{8,9},{9,10},{10,1... | collective-permute-start | bytes 786440 | tf_op jit(solution)/shard_map/ppermute | solution.py:27
  133.2 14.1 %collective-permute-start.21 = (f32[320,128]{1,0:T(8,128)S(1)}, f32[320,128]{1,0:T(8,128)S(1)}, u32[]{:S(2)}, u32[]{:S(2)}) collective-permute-start(f32[320,128]{1,0:T(8,128)S(1)} %broadcast_select_fusion.p0), channel_id=1, source_target_pairs={{0,1},{1,2},{2,3},{3,0},{4,5},{5,6},{6,7},{7,4},{8,9},{9,10},{10,1... | collective-permute-start | bytes 491528 | tf_op jit(solution)/shard_map/ppermute | solution.py:27
  171.8 0.7 copy-start.5
  172.5 0.7 copy-start.7
  173.2 0.7 copy-start.9
  173.9 0.7 copy-start.3
  174.7 2.2 %copy-start.1 = (f32[1,512,2048]{2,1,0:T(8,128)S(1)}, f32[1,512,2048]{2,1,0:T(8,128)}, u32[]{:S(2)}) copy-start(f32[1,512,2048]{2,1,0:T(8,128)} %param.4) | copy-start | bytes 12582916
  176.9 2.2 %copy-start.2 = (f32[2048,512]{1,0:T(8,128)S(1)}, f32[2048,512]{1,0:T(8,128)}, u32[]{:S(2)}) copy-start(f32[2048,512]{1,0:T(8,128)} %all-gather.2.cloned.1.call-done.a_col) | copy-start | bytes 12582916
  179.0 1.0 copy-start.4
  180.0 0.9 copy-start.6
  181.0 0.9 copy-start.8
  181.9 0.9 copy-start.10
Sparse Core Ops, SparseCore 0:
  66.3 53.7 all-gather.1

commit v2 on v1

v2 whole, which is shorter than its diff:
```python
import jax
import jax.numpy as jnp
from jax import lax
from jax.experimental import pallas as pl
from jax.experimental.pallas import tpu as pltpu
from jax.sharding import PartitionSpec as P

BLOCK = 128
PANEL = 512
FRONTS, ROWS, COLS = 4, 16, 4
AXES = ("front", "row", "col")
HIGHEST = lax.Precision.HIGHEST
MIB = 2**20


def permute(x, route):
    def flat(f, r, c):
        return (f * ROWS + r) * COLS + c

    pairs = []
    for f in range(FRONTS):
        for r in range(ROWS):
            for c in range(COLS):
                target = route(f, r, c)
                if target is not None:
                    pairs.append((flat(f, r, c), flat(*target)))
    return lax.ppermute(x, AXES, pairs)


def dot(a, b, ca, cb):
    return lax.dot_general(
        a, b, (((ca,), (cb,)), ((), ())), precision=HIGHEST, preferred_element_type=jnp.float32
    )


def smem():
    return pl.BlockSpec(memory_space=pltpu.SMEM)


def hbm():
    return pl.BlockSpec(memory_space=pltpu.HBM)


def whole(shape):
    return pl.BlockSpec(shape, lambda i: (0,) * len(shape))


def place(dst, col_off, bmap, run, rows, cols, tile):
    for row_id, row_part in rows:
        t = bmap[0, row_id]
        for col_id, fetch in cols:
            u = bmap[0, col_id]

            @pl.when((t // 4 == run) & (u // 4 == tile))
            def _():
                at_r = pl.ds(pl.multiple_of((t % 4) * BLOCK, BLOCK), BLOCK)
                at_c = pl.ds(pl.multiple_of(col_off + (u % 4) * BLOCK, BLOCK), BLOCK)
                dst[at_r, at_c] = dst[at_r, at_c] + fetch(row_part)


def pack_kernel(left, right, block, ea, eb, ed, ee, top, bottom):
    top[...] = block[:BLOCK, :]
    bottom[...] = block[BLOCK:, :]
    ea[...] = left[:BLOCK, :]
    eb[...] = left[...]
    ed[...] = right[:BLOCK, :]
    ee[...] = right[...]


def pack_call(child):
    shapes = [(128, 128), (256, 128), (128, 256), (256, 256), (128, 1024), (128, 1024)]
    return pl.pallas_call(
        pack_kernel,
        grid=(1,),
        in_specs=[
            pl.BlockSpec((256, 128), lambda i: (0, 0)),
            pl.BlockSpec((256, 256), lambda i: (0, 3)),
            pl.BlockSpec((256, 1024), lambda i: (0, 0)),
        ],
        out_specs=[whole(x) for x in shapes],
        out_shape=[jax.ShapeDtypeStruct(x, jnp.float32) for x in shapes],
        name="pack",
    )(child, child, child)


def panel_kernel(bmap, order, front, ea, eb, ed, ee, q0, q1, q2, q3, work):
    r = lax.axis_index("row")
    work[...] = front[...]

    def left(part):
        return ea[...] if part == 0 else eb[(part - 1) * BLOCK : part * BLOCK, :]

    def right(which):
        at = slice(which * BLOCK, (which + 1) * BLOCK)

        def fetch(part):
            return ed[:, at] if part == 0 else ee[(part - 1) * BLOCK : part * BLOCK, at]

        return fetch

    rows = [(2 * r, 0), ((2 * r + 30) % 32, 1), ((2 * r + 31) % 32, 2)]
    cols = [(0, left), (30, right(0)), (31, right(1))]
    place(work, 0, bmap, r, rows, cols, 0)
    for q, out in enumerate((q0, q1, q2, q3)):
        index = r * 512 + q * BLOCK + lax.broadcasted_iota(jnp.int32, out.shape, 0)
        out[...] = jnp.where(index < order[0], work[q * BLOCK : (q + 1) * BLOCK, :], 0.0)


def panel_call(bmap, order, front, *pieces):
    return pl.pallas_call(
        panel_kernel,
        grid=(1,),
        in_specs=[smem(), smem(), whole((512, 512))] + [whole(p.shape) for p in pieces],
        out_specs=[whole((128, 512))] * 4,
        out_shape=[jax.ShapeDtypeStruct((128, 512), jnp.float32)] * 4,
        scratch_shapes=[pltpu.VMEM((512, 512), jnp.float32)],
        compiler_params=pltpu.CompilerParams(vmem_limit_bytes=16 * MIB),
        name="panel",
    )(bmap, order, front, *pieces)


def reciprocal(d):
    r = pl.reciprocal(d, approx=True)
    r = r * (2.0 - d * r)
    return r * (2.0 - d * r)


def sweep(groups):
    lane = lax.broadcasted_iota(jnp.int32, (8, 128), 1)
    sub = lax.broadcasted_iota(jnp.int32, (8, 128), 0)
    w = list(groups)

    def across(v, k):
        return jnp.broadcast_to(v[:, k : k + 1], (8, 128))

    def down(v, k):
        return jnp.broadcast_to(v[k : k + 1, :], (8, 128))

    for g in range(16):
        base = 8 * g
        top = w[g]
        col = [across(top, base + j) for j in range(8)]
        inverse, pivot = [], {}
        for j in range(8):
            inverse.append(reciprocal(down(col[j], j)))
            m = jnp.where(sub > j, col[j] * inverse[j], 0.0)
            row = jnp.where(lane == base + j, 1.0, down(top, j))
            top = jnp.where((lane == base + j) & (sub > j), 0.0, top) - m * row
            for q in range(j + 1, 8):
                pivot[j, q] = down(col[q], j)
                col[q] = col[q] - m * pivot[j, q]
        w[g] = top
        inside = (lane >= base) & (lane < base + 8)
        rows = []
        for j in range(8):
            later = (lane > base + j) & (lane < base + 8)
            rows.append(jnp.where(lane == base + j, 1.0, jnp.where(later, 0.0, down(top, j))))
        for h in range(g + 1, 16):
            c = [across(w[h], base + j) for j in range(8)]
            acc = jnp.where(inside, 0.0, w[h])
            for j in range(8):
                m = c[j] * inverse[j]
                for q in range(j + 1, 8):
                    c[q] = c[q] - m * pivot[j, q]
                acc = acc - m * rows[j]
            w[h] = acc
    return w


def gather_rows(dst, parts):
    c = lax.axis_index("col")
    rows = dst.shape[0] // 4
    for s, p in enumerate(parts):
        at = pl.ds(pl.multiple_of(((c + 4 - s) % 4) * rows, rows), rows)
        dst[at, :] = p[...]


def invert(work, out, low):
    ri = lax.broadcasted_iota(jnp.int32, (BLOCK, BLOCK), 0)
    ci = lax.broadcasted_iota(jnp.int32, (BLOCK, BLOCK), 1)

    def step(j, carry):
        off = pl.multiple_of(j * BLOCK, BLOCK)
        groups = [
            work[pl.ds(pl.multiple_of(off + 8 * g, 8), 8), pl.ds(off, BLOCK)] for g in range(16)
        ]
        w = jnp.concatenate(sweep(groups), axis=0)
        scale = lax.rsqrt(jnp.sum(jnp.where(ri == ci, w, 0.0), axis=1, keepdims=True))
        inv = jnp.where(ri > ci, w, jnp.where(ri == ci, 1.0, 0.0)) * scale
        out[pl.ds(off, BLOCK), pl.ds(off, BLOCK)] = inv

        @pl.when(j == 0)
        def _():
            below = dot(work[BLOCK:, :BLOCK], inv, 1, 1)
            work[BLOCK:, BLOCK:] = work[BLOCK:, BLOCK:] - dot(below, below, 1, 1)
            low[...] = below

        @pl.when(j == 1)
        def _():
            out[BLOCK:, :BLOCK] = -dot(inv, dot(low[...], out[:BLOCK, :BLOCK], 1, 0), 1, 0)
            out[:BLOCK, BLOCK:] = jnp.zeros((BLOCK, BLOCK), jnp.float32)

        return carry

    lax.fori_loop(0, 2, step, 0)


HALF = (256, 256)


def first_kernel(q0, q1, q2, q3, inv, below, rest, work, low):
    work[:BLOCK, :] = q0[:, :256]
    work[BLOCK:, :] = q1[:, :256]
    invert(work, inv, low)
    x = dot(jnp.concatenate([q2[:, :256], q3[:, :256]], axis=0), inv[...], 1, 1)
    below[...] = x
    rest[...] = jnp.concatenate([q2[:, 256:], q3[:, 256:]], axis=0) - dot(x, x, 1, 1)


def first_call(quarter):
    return pl.pallas_call(
        first_kernel,
        grid=(1,),
        in_specs=[whole((128, 512))] * 4,
        out_specs=[whole(HALF)] * 3,
        out_shape=[jax.ShapeDtypeStruct(HALF, jnp.float32)] * 3,
        scratch_shapes=[pltpu.VMEM(HALF, jnp.float32), pltpu.VMEM((BLOCK, BLOCK), jnp.float32)],
        compiler_params=pltpu.CompilerParams(vmem_limit_bytes=16 * MIB),
        cost_estimate=pl.CostEstimate(flops=10**10, bytes_accessed=4 * MIB, transcendentals=0),
        name="first",
    )(*quarter)


def second_kernel(inv, below, rest, k0, k1, k2, k3, work, out, low, packed):
    work[...] = rest[...]
    invert(work, out, low)
    corner = -dot(out[...], dot(below[...], inv[...], 1, 0), 1, 0)
    spots = [(inv, 0, 0), (inv, 1, 0), (inv, 1, 1), (out, 0, 0), (out, 1, 0), (out, 1, 1)]
    for k, (src, i, j) in enumerate(spots):
        packed[k * BLOCK : (k + 1) * BLOCK, :] = src[
            i * BLOCK : (i + 1) * BLOCK, j * BLOCK : (j + 1) * BLOCK
        ]
    packed[768:1024, :] = corner[:, :BLOCK]
    packed[1024:, :] = corner[:, BLOCK:]
    for q, k in enumerate((k0, k1, k2, k3)):
        k[...] = packed[q * 320 : (q + 1) * 320, :]


def unpack(linv, packed):
    linv[...] = jnp.zeros_like(linv)
    for k, (i, j) in enumerate(((0, 0), (1, 0), (1, 1), (2, 2), (3, 2), (3, 3))):
        linv[i * BLOCK : (i + 1) * BLOCK, j * BLOCK : (j + 1) * BLOCK] = packed[
            k * BLOCK : (k + 1) * BLOCK, :
        ]
    linv[256:, :BLOCK] = packed[768:1024, :]
    linv[256:, BLOCK:256] = packed[1024:, :]


def second_call(inv, below, rest):
    part = (320, 128)
    return pl.pallas_call(
        second_kernel,
        grid=(1,),
        in_specs=[whole(HALF)] * 3,
        out_specs=[whole(part)] * 4,
        out_shape=[jax.ShapeDtypeStruct(part, jnp.float32)] * 4,
        scratch_shapes=[
            pltpu.VMEM(HALF, jnp.float32),
            pltpu.VMEM(HALF, jnp.float32),
            pltpu.VMEM((BLOCK, BLOCK), jnp.float32),
            pltpu.VMEM((1280, 128), jnp.float32),
        ],
        compiler_params=pltpu.CompilerParams(vmem_limit_bytes=16 * MIB),
        cost_estimate=pl.CostEstimate(flops=10**10, bytes_accessed=4 * MIB, transcendentals=0),
        name="second",
    )(inv, below, rest)


def halves(x):
    high = x.astype(jnp.bfloat16)
    return high, (x - high.astype(jnp.float32)).astype(jnp.bfloat16)


def dot3(a_high, a_low, b_high, b_low):
    def part(x, y):
        return lax.dot_general(
            x, y, (((1,), (1,)), ((), ())), preferred_element_type=jnp.float32
        )

    return part(a_high, b_high) + (part(a_high, b_low) + part(a_low, b_high))


def update_kernel(
    bmap, order, l0, l1, l2, l3, a0, a1, a2, a3, front, own, prev0, prev1, edge0, edge1, a_col,
    x_out, s_out, packed, linv, a_row, x_buf, z_high, z_low, child, tiles, cols, front_sem, col_sem, child_sem, x_sem, s_sem,
):
    r = lax.axis_index("row")
    c = lax.axis_index("col")
    wide = child.shape[1]

    def columns(t):
        return pl.ds(pl.multiple_of(t * 512, 512), 512)

    def front_copy(t):
        return pltpu.make_async_copy(front.at[:, columns(t)], tiles.at[t], front_sem.at[t])

    def col_copy(t):
        return pltpu.make_async_copy(a_col.at[columns(t), :], cols.at[t], col_sem.at[t])

    def out_copy(t):
        return pltpu.make_async_copy(tiles.at[t], s_out.at[:, columns(t)], s_sem.at[t])

    upper, rest = pl.ds(0, BLOCK), pl.ds(BLOCK, 2 * BLOCK)
    middle, lower = pl.ds(BLOCK, BLOCK), pl.ds(2 * BLOCK, BLOCK)
    left, right = pl.ds(0, 2 * BLOCK), pl.ds(2 * BLOCK, wide - 2 * BLOCK)
    child_copies = [
        pltpu.make_async_copy(src, child.at[at], child_sem.at[k])
        for k, (src, at) in enumerate(
            [
                (own, (upper, right)),
                (prev0, (middle, right)),
                (prev1, (lower, right)),
                (edge0, (upper, left)),
                (edge1, (rest, left)),
            ]
        )
    ]
    front_copy(0).start()
    for copy in child_copies:
        copy.start()
    col_copy(0).start()
    for t in range(1, 4):
        front_copy(t).start()
        col_copy(t).start()

    gather_rows(packed, (l0, l1, l2, l3))
    unpack(linv, packed)
    gather_rows(a_row, (a0, a1, a2, a3))
    x = dot(a_row[...], linv[...], 1, 1)
    x_buf[...] = x
    x_copy = pltpu.make_async_copy(x_buf, x_out, x_sem)
    x_copy.start()
    high, low = halves(dot(x, linv[...], 1, 0))
    z_high[...] = high
    z_low[...] = low
    for copy in child_copies:
        copy.wait()

    rows = [(2 * r, 0), ((2 * r + 30) % 32, 1), ((2 * r + 31) % 32, 2)]
    row = r * 512 + lax.broadcasted_iota(jnp.int32, (512, 1), 0)

    def step(t, carry):
        front_copy(t).wait()
        tile = tiles.at[t]

        def block(k):
            at = pl.ds(pl.multiple_of((2 * t + k) * BLOCK, BLOCK), BLOCK)
            return lambda part: child[part * BLOCK : (part + 1) * BLOCK, at]

        ids = [((8 * c + 2 * t + 30 + k) % 32, block(k)) for k in range(3)]
        place(tile, 0, bmap, r, rows, ids, 4 * c + t)
        col_copy(t).wait()
        col = (4 * c + t) * 512 + lax.broadcasted_iota(jnp.int32, (1, 512), 1)
        keep = (row >= PANEL) & (row < order[0]) & (col >= PANEL) & (col < order[0])
        product = dot3(z_high[...], z_low[...], *halves(cols[t]))
        tile[...] = jnp.where(keep, tile[...] - product, 0.0)
        out_copy(t).start()
        return carry

    lax.fori_loop(0, 4, step, 0)
    x_copy.wait()
    for t in range(4):
        out_copy(t).wait()


def update_call(bmap, order, l_parts, a_parts, front, own, prev0, prev1, edge0, edge1, a_col):
    square = (512, 512)
    return pl.pallas_call(
        update_kernel,
        grid=(1,),
        in_specs=[smem(), smem()]
        + [whole((320, 128))] * 4
        + [whole((128, 512))] * 4
        + [hbm()] * 7,
        out_specs=[hbm(), hbm()],
        out_shape=[
            jax.ShapeDtypeStruct(square, jnp.float32),
            jax.ShapeDtypeStruct((512, 2048), jnp.float32),
        ],
        scratch_shapes=[
            pltpu.VMEM((1280, 128), jnp.float32),
            pltpu.VMEM(square, jnp.float32),
            pltpu.VMEM(square, jnp.float32),
            pltpu.VMEM(square, jnp.float32),
            pltpu.VMEM(square, jnp.bfloat16),
            pltpu.VMEM(square, jnp.bfloat16),
            pltpu.VMEM((384, 1280), jnp.float32),
            pltpu.VMEM((4, 512, 512), jnp.float32),
            pltpu.VMEM((4, 512, 512), jnp.float32),
            pltpu.SemaphoreType.DMA((4,)),
            pltpu.SemaphoreType.DMA((4,)),
            pltpu.SemaphoreType.DMA((5,)),
            pltpu.SemaphoreType.DMA,
            pltpu.SemaphoreType.DMA((4,)),
        ],
        compiler_params=pltpu.CompilerParams(vmem_limit_bytes=60 * MIB),
        name="update",
    )(bmap, order, *l_parts, *a_parts, front, own, prev0, prev1, edge0, edge1, a_col)


def after(x, *earlier):
    return lax.optimization_barrier((x, *earlier))[0]


def body(front_matrix, child_update, bmap, order):
    front = front_matrix[0]
    child = child_update[0]
    row = lax.axis_index("row")
    c = lax.axis_index("col")

    ea, eb, e0, e1, top, bottom = pack_call(child)
    ee = permute(e1, lambda f, r, c: (f ^ 1, (r + 1) % ROWS, 0) if c == 3 else None)
    ed = permute(e0, lambda f, r, c: (f ^ 1, r, 0) if c == 3 else None)
    eb = permute(eb, lambda f, r, c: (f ^ 1, (r + 1) % ROWS, 0) if c == 0 else None)
    ea = permute(ea, lambda f, r, c: (f ^ 1, r, 0) if c == 0 else None)
    quarter = panel_call(bmap, order, front[:, :PANEL], ea, eb, ed, ee)

    def across(x):
        return permute(x, lambda f, r, c: (f ^ 1, r, c))

    top, bottom, e0, e1, _ = lax.optimization_barrier((top, bottom, e0, e1, quarter[0]))
    own = across(top)
    prev1 = permute(bottom, lambda f, r, c: (f, (r + 1) % ROWS, c))

    got = [
        permute(quarter[q], lambda f, r, c, q=q: (f, r, q) if c == 0 else None) for q in (1, 2, 3)
    ]

    half = first_call(quarter)
    *got, own, prev1, e0, e1, _ = lax.optimization_barrier((*got, own, prev1, e0, e1, half[0]))
    prev1 = across(prev1)
    prev0 = permute(own, lambda f, r, c: (f, (r + 1) % ROWS, c))
    edge0 = permute(e0, lambda f, r, c: (f, r, (c + 1) % COLS))
    edge1 = permute(e1, lambda f, r, c: (f, (r + 1) % ROWS, (c + 1) % COLS))
    mine = jnp.where(c == 0, quarter[0], got[0] + got[1] + got[2])

    piece = permute(mine, lambda f, r, c: (f, 4 * (r % 4) + c, r // 4))

    *half, _, _ = lax.optimization_barrier((*half, mine, own))
    part = second_call(*half)
    piece, prev0, prev1, edge0, edge1, *part = lax.optimization_barrier(
        (piece, prev0, prev1, edge0, edge1, *part)
    )
    edge0, edge1 = across(edge0), across(edge1)
    a_col = lax.all_gather(piece, "row", axis=0, tiled=True)

    got = [
        permute(part[q], lambda f, r, c, q=q: (f, 0, q) if r == 0 and c == 0 else None)
        for q in (1, 2, 3)
    ]
    d = jnp.where(c == 0, part[0], got[0] + got[1] + got[2])

    m = after(mine, part[0])
    a_parts = [permute(m, lambda f, r, c, s=s: (f, r, (c + s) % COLS)) for s in (1, 2, 3)]

    d1 = permute(d, lambda f, r, c: (f, 6, c) if r == 0 else None)
    d2 = permute(d, lambda f, r, c: (f, 12, c) if r == 0 else None)
    d = jnp.where(row == 0, d, d1 + d2)
    d, *a_parts = lax.optimization_barrier((d, *a_parts))
    a_parts = [mine, *a_parts]
    d1 = permute(d, lambda f, r, c: (f, (r + 2) % ROWS, c) if r in (0, 6, 12) else None)
    d2 = permute(d, lambda f, r, c: (f, r - 2, c) if r in (6, 12) else None)
    d = jnp.where((row == 0) | (row == 6) | (row == 12), d, d1 + d2)
    d1 = permute(d, lambda f, r, c: (f, r + 1, c) if r % 2 == 0 else None)
    d = jnp.where(row % 2 == 0, d, d1)
    l_parts = [d] + [permute(d, lambda f, r, c, s=s: (f, r, (c + s) % COLS)) for s in (1, 2, 3)]

    x, s = update_call(bmap, order, l_parts, a_parts, front, own, prev0, prev1, edge0, edge1, a_col)
    return x[None], s[None]


def solution(mesh):
    return jax.shard_map(
        body,
        mesh=mesh,
        in_specs=(P("front", "row", "col"), P("front", "row", "col"), P("front", None), P("front")),
        out_specs=(P("front", "row", None), P("front", "row", "col")),
        check_vma=False,
    )
```

time: 206 us -> 142 us (0.69)
  waiting for transfers between devices: 80 us -> 42 us
  local copies, waits for them, and re-layouts: 17.7 us -> 2.02 us
  starting transfers between devices: 50.6 us -> 42.1 us
    ppermute x28 -> x30, waiting for transfers between devices: 80 us -> 42 us  [permute(): return lax.ppermute(x, AXES, pairs)]
    unnamed x26 -> x32, local copies, waits for them, and re-layouts: 13.9 us -> 0.72 us
    ppermute x28 -> x30, starting transfers between devices: 50.6 us -> 42.1 us  [permute(): return lax.ppermute(x, AXES, pairs)]
    slice x8 -> x1, local copies, waits for them, and re-layouts: 3.76 us -> 1.3 us  [body(): quarter = panel_call(bmap, order, front[:, :PANEL], ea, eb, ed, ee)]
    pallas_call x3 -> x5, Pallas kernels: 39.4 us -> 39.8 us  [the longest x1 12.4 us: first_call(): pl.pallas_call(first_kernel, grid=(1,), in_specs=[whole((128, 512))] * 4,...]
  transfers between devices with their start and end apart: 29 -> 31, of which waited for: 10 -> 10; matrix products, arithmetic and copies ran while one was open for 1% -> 1% of each run, Pallas kernels for 12% -> 17%
where the time goes in v2:
time: 142 us; the launch traced here: 141 us
  starting transfers between devices  42.1 us (30%)
  waiting for transfers between devices  42 us (30%)
  Pallas kernels  39.8 us (28%)
  between operations  15.2 us (11%)
  local copies, waits for them, and re-layouts  2.02 us (1%)
    ppermute x30, starting transfers between devices, permute(): return lax.ppermute(x, AXES, pairs)  42.1 us
    ppermute x30, waiting for transfers between devices, permute(): return lax.ppermute(x, AXES, pairs)  42 us
    pallas_call x1, Pallas kernels, first_call(): pl.pallas_call(first_kernel, grid=(1,), in_specs=[whole((128, 512))] * 4,...  12.4 us
    pallas_call x1, Pallas kernels, second_call(): pl.pallas_call(second_kernel, grid=(1,), in_specs=[whole(HALF)] * 3, out_...  12.3 us
    pallas_call x1, Pallas kernels, update_call(): pl.pallas_call(update_kernel, grid=(1,), in_specs=[smem(), smem()] + [who...  11.7 us
  transfers between devices with their start and end apart: 31, of which 10 were waited for; matrix products, arithmetic and copies ran while one was open for 1% of the time, Pallas kernels for 17%

profile of v2, /device:TPU:1, one launch (start us, length us, event | category | flops | bytes accessed | tf_op | source)
XLA Modules:
  0.0 141.3 jit_solution(8801734135353346315)
XLA Ops:
  7.2 0.0 copy-start
  7.2 0.0 all-gather.2.cloned.1.call-start
  7.2 2.5 %pack.1 = (f32[128,128]{1,0:T(8,128)}, f32[256,128]{1,0:T(8,128)}, f32[128,256]{1,0:T(8,128)}, f32[256,256]{1,0:T(8,128)}, f32[128,1024]{1,0:T(8,128)}, /*index=5*/f32[128,1024]{1,0:T(8,128)}) custom-call(f32[256,1024]{1,0:T(8,128)} %bitcast.4, f32[256,1024]{1,0:T(8,128)} %bitcast.5, f32[256,1024]{1,0:T(8,128)} %bitcast.6), custom_call_target="tpu_custom_call" | custom-call | tf_op jit(solution)/shard_map/pack/pallas_call | solution.py:72
  9.8 1.3 collective-permute-start.3
  11.1 5.9 %collective-permute-start.1 = (f32[256,128]{1,0:T(8,128)}, f32[256,128]{1,0:T(8,128)S(1)}, u32[]{:S(2)}, u32[]{:S(2)}) collective-permute-start(f32[256,128]{1,0:T(8,128)} %get-tuple-element.50), channel_id=1, source_target_pairs={{0,68},{4,72},{8,76},{12,80},{16,84},{20,88},{24,92},{28,96},{32,1... | collective-permute-start | bytes 393224 | tf_op jit(solution)/shard_map/ppermute | solution.py:27
  16.9 1.3 collective-permute-start.2
  18.2 2.2 %collective-permute-start = (f32[128,128]{1,0:T(8,128)}, f32[128,128]{1,0:T(8,128)S(1)}, u32[]{:S(2)}, u32[]{:S(2)}) collective-permute-start(f32[128,128]{1,0:T(8,128)} %get-tuple-element.49), channel_id=1, source_target_pairs={{0,64},{4,68},{8,72},{12,76},{16,80},{20,84},{24,88},{28,92},{32,9... | collective-permute-start | bytes 196616 | tf_op jit(solution)/shard_map/ppermute | solution.py:27
  21.0 1.3 slice.4.front
  22.3 2.2 %collective-permute-done.ea = f32[128,128]{1,0:T(8,128)S(1)} collective-permute-done((f32[128,128]{1,0:T(8,128)}, f32[128,128]{1,0:T(8,128)S(1)}, u32[]{:S(2)}, u32[]{:S(2)}) %collective-permute-start) | collective-permute-done | bytes 65568 | tf_op jit(solution)/shard_map/ppermute | solution.py:27
  24.6 0.0 collective-permute-done.1.eb
  24.6 3.3 %collective-permute-done.2.ed = f32[128,256]{1,0:T(8,128)S(1)} collective-permute-done((f32[128,256]{1,0:T(8,128)}, f32[128,256]{1,0:T(8,128)S(1)}, u32[]{:S(2)}, u32[]{:S(2)}) %collective-permute-start.2) | collective-permute-done | bytes 131104 | tf_op jit(solution)/shard_map/ppermute | solution.py:27
  27.9 0.0 collective-permute-done.3.ee
  27.9 0.9 panel.1
  28.7 1.3 collective-permute-start.4
  30.1 1.3 collective-permute-start.5
  31.4 1.4 %collective-permute-start.6 = (f32[128,512]{1,0:T(8,128)S(1)}, f32[128,512]{1,0:T(8,128)S(1)}, u32[]{:S(2)}, u32[]{:S(2)}) collective-permute-start(f32[128,512]{1,0:T(8,128)S(1)} %get-tuple-element.56.q3), channel_id=1, source_target_pairs={{0,3},{4,7},{8,11},{12,15},{16,19},{20,23},{24,27},{28,31},{32,35}... | collective-permute-start | bytes 786440 | tf_op jit(solution)/shard_map/ppermute | solution.py:27
  32.8 0.3 collective-permute-start.7
  33.1 1.9 %collective-permute-start.8 = (f32[128,1024]{1,0:T(8,128)}, f32[128,1024]{1,0:T(8,128)S(1)}, u32[]{:S(2)}, u32[]{:S(2)}) collective-permute-start(f32[128,1024]{1,0:T(8,128)} %get-tuple-element.60), channel_id=1, source_target_pairs={{0,4},{1,5},{2,6},{3,7},{4,8},{5,9},{6,10},{7,11},{8,12},{9,13},{1... | collective-permute-start | bytes 1572872 | tf_op jit(solution)/shard_map/ppermute | solution.py:27
  35.0 12.4 %first.1 = (f32[256,256]{1,0:T(8,128)S(1)}, f32[256,256]{1,0:T(8,128)S(1)}, f32[256,256]{1,0:T(8,128)S(1)}) custom-call(f32[128,512]{1,0:T(8,128)S(1)} %get-tuple-element.53.q0, f32[128,512]{1,0:T(8,128)S(1)} %get-tuple-element.54.q1, f32[128,512]{1,0:T(8,128)S(1)} %get-tuple-element.55.q2, f32[128,512]{1,0:T(8,128)S(1)} %get-tuple-element.56.q3), custom_call_target="tpu_custom_call" | custom-call | flops 10000000000 | bytes 4194304 | tf_op jit(solution)/shard_map/first/pallas_call | solution.py:221
  47.3 0.0 collective-permute-done.5
  47.4 0.0 collective-permute-done.6
  47.4 0.0 collective-permute-done.8
  47.4 0.1 add_select_fusion.a0
  47.5 3.3 %collective-permute-start.9 = (f32[128,512]{1,0:T(8,128)S(1)}, f32[128,512]{1,0:T(8,128)S(1)}, u32[]{:S(2)}, u32[]{:S(2)}) collective-permute-start(f32[128,512]{1,0:T(8,128)S(1)} %add_select_fusion.a0), channel_id=1, source_target_pairs={{0,0},{1,4},{2,8},{3,12},{4,16},{5,20},{6,24},{7,28},{8,32},{9,36}... | collective-permute-start | bytes 786440 | tf_op jit(solution)/shard_map/ppermute | solution.py:27
  50.8 4.5 %collective-permute-start.10 = (f32[128,1024]{1,0:T(8,128)S(1)}, f32[128,1024]{1,0:T(8,128)S(1)}, u32[]{:S(2)}, u32[]{:S(2)}) collective-permute-start(f32[128,1024]{1,0:T(8,128)S(1)} %collective-permute-done.7.own), channel_id=1, source_target_pairs={{0,4},{1,5},{2,6},{3,7},{4,8},{5,9},{6,10},{7,11},{8,12},{9,13},{1... | collective-permute-start | bytes 1572872 | tf_op jit(solution)/shard_map/ppermute | solution.py:27
  55.3 1.9 %collective-permute-start.12 = (f32[128,256]{1,0:T(8,128)S(1)}, f32[128,256]{1,0:T(8,128)S(1)}, u32[]{:S(2)}, u32[]{:S(2)}) collective-permute-start(f32[128,256]{1,0:T(8,128)S(1)} %copy-done.15), channel_id=1, source_target_pairs={{0,1},{1,2},{2,3},{3,0},{4,5},{5,6},{6,7},{7,4},{8,9},{9,10},{10,1... | collective-permute-start | bytes 393224 | tf_op jit(solution)/shard_map/ppermute | solution.py:27
  57.2 1.0 collective-permute-start.13
  58.2 0.2 collective-permute-start.11
  58.4 12.3 %second.1 = (f32[320,128]{1,0:T(8,128)S(1)}, f32[320,128]{1,0:T(8,128)S(1)}, f32[320,128]{1,0:T(8,128)S(1)}, f32[320,128]{1,0:T(8,128)S(1)}) custom-call(f32[256,256]{1,0:T(8,128)S(1)} %get-tuple-element.73.inv, f32[256,256]{1,0:T(8,128)S(1)} %get-tuple-element.74.below, f32[256,256]{1,0:T(8,128)S(1)} %get-tuple-element.75.rest), custom_call_target="tpu_custom_call" | custom-call | flops 10000000000 | bytes 4194304 | tf_op jit(solution)/shard_map/second/pallas_call | solution.py:261
  70.8 0.0 collective-permute-done.9
  70.8 0.0 copy-start.10
  70.8 0.6 collective-permute-done.11.prev1
  71.4 0.0 collective-permute-done.10.prev0
  71.4 0.1 copy-done.10
  71.5 0.0 all-gather.2.cloned.1.call-update
  71.5 0.7 collective-permute-start.14
  72.2 0.7 collective-permute-start.15
  72.9 0.7 collective-permute-start.16
  73.6 0.0 collective-permute-done.16
  73.6 0.7 collective-permute-start.18
  74.3 0.7 collective-permute-start.17
  75.0 1.9 %collective-permute-start.21 = (f32[128,512]{1,0:T(8,128)S(1)}, f32[128,512]{1,0:T(8,128)S(1)}, u32[]{:S(2)}, u32[]{:S(2)}) collective-permute-start(f32[128,512]{1,0:T(8,128)S(1)} %add_select_fusion.a0), channel_id=1, source_target_pairs={{0,3},{1,0},{2,1},{3,2},{4,7},{5,4},{6,5},{7,6},{8,11},{9,8},{10,9... | collective-permute-start | bytes 786440 | tf_op jit(solution)/shard_map/ppermute | solution.py:27
  76.9 1.6 %collective-permute-start.20 = (f32[128,512]{1,0:T(8,128)S(1)}, f32[128,512]{1,0:T(8,128)S(1)}, u32[]{:S(2)}, u32[]{:S(2)}) collective-permute-start(f32[128,512]{1,0:T(8,128)S(1)} %add_select_fusion.a0), channel_id=1, source_target_pairs={{0,2},{1,3},{2,0},{3,1},{4,6},{5,7},{6,4},{7,5},{8,10},{9,11},{10,... | collective-permute-start | bytes 786440 | tf_op jit(solution)/shard_map/ppermute | solution.py:27
  78.5 0.0 collective-permute-start.19
  78.5 0.0 collective-permute-done.17
  78.5 4.8 %collective-permute-done.21.a3 = f32[128,512]{1,0:T(8,128)S(1)} collective-permute-done((f32[128,512]{1,0:T(8,128)S(1)}, f32[128,512]{1,0:T(8,128)S(1)}, u32[]{:S(2)}, u32[]{:S(2)}) %collective-permute-start.21) | collective-permute-done | bytes 262176 | tf_op jit(solution)/shard_map/ppermute | solution.py:27
  83.4 0.3 collective-permute-done.20.a2
  83.7 2.7 %collective-permute-done.19.a1 = f32[128,512]{1,0:T(8,128)S(1)} collective-permute-done((f32[128,512]{1,0:T(8,128)S(1)}, f32[128,512]{1,0:T(8,128)S(1)}, u32[]{:S(2)}, u32[]{:S(2)}) %collective-permute-start.19) | collective-permute-done | bytes 262176 | tf_op jit(solution)/shard_map/ppermute | solution.py:27
  86.5 0.7 collective-permute-start.23
  87.1 0.7 collective-permute-start.22
  87.8 0.0 collective-permute-done.23
  87.8 0.0 collective-permute-done.22
  87.9 1.3 collective-permute-start.24
  89.2 1.3 collective-permute-start.29
  90.4 19.3 %collective-permute-done.24 = f32[320,128]{1,0:T(8,128)S(1)} collective-permute-done((f32[320,128]{1,0:T(8,128)S(1)}, f32[320,128]{1,0:T(8,128)S(1)}, u32[]{:S(2)}, u32[]{:S(2)}) %collective-permute-start.24) | collective-permute-done | bytes 163872 | tf_op jit(solution)/shard_map/ppermute | solution.py:27
  109.8 1.8 %collective-permute-start.27 = (f32[320,128]{1,0:T(8,128)S(1)}, f32[320,128]{1,0:T(8,128)S(1)}, u32[]{:S(2)}, u32[]{:S(2)}) collective-permute-start(f32[320,128]{1,0:T(8,128)S(1)} %broadcast_select_fusion.l0), channel_id=1, source_target_pairs={{0,3},{1,0},{2,1},{3,2},{4,7},{5,4},{6,5},{7,6},{8,11},{9,8},{10,9... | collective-permute-start | bytes 491528 | tf_op jit(solution)/shard_map/ppermute | solution.py:27
  111.6 0.7 collective-permute-start.25
  112.3 1.2 collective-permute-start.28
  113.4 3.1 %collective-permute-done.28.edge0 = f32[128,256]{1,0:T(8,128)S(1)} collective-permute-done((f32[128,256]{1,0:T(8,128)S(1)}, f32[128,256]{1,0:T(8,128)S(1)}, u32[]{:S(2)}, u32[]{:S(2)}) %collective-permute-start.28) | collective-permute-done | bytes 131104 | tf_op jit(solution)/shard_map/ppermute | solution.py:27
  116.6 0.0 collective-permute-done.27.l3
  116.6 1.2 collective-permute-done.26.l2
  117.9 4.2 %collective-permute-done.25.l1 = f32[320,128]{1,0:T(8,128)S(1)} collective-permute-done((f32[320,128]{1,0:T(8,128)S(1)}, f32[320,128]{1,0:T(8,128)S(1)}, u32[]{:S(2)}, u32[]{:S(2)}) %collective-permute-start.25) | collective-permute-done | bytes 163872 | tf_op jit(solution)/shard_map/ppermute | solution.py:27
  122.2 0.6 copy-done.13
  122.7 11.7 %update.1 = (f32[512,512]{1,0:T(8,128)}, f32[512,2048]{1,0:T(8,128)}) custom-call(s32[1,32]{1,0:T(1,128)} %bmap.3, s32[1]{0:T(128)S(6)} %copy.6.order, f32[320,128]{1,0:T(8,128)} %copy-done.2, f32[320,128]{1,0:T(8,128)} %copy-done.13, f32[320,128]{1,0:T(8,128)} %copy-done.12, f32[320,128]{1,0:T(8,128)} %copy-done.11, f32[128,512]{1,0:T(8,128)} %copy-done.1, ...), custom_call_target="tpu_custom_call" | custom-call | tf_op jit(solution)/shard_map/update/pallas_call | solution.py:378
  (42 shorter events, 0.2 us)
Async XLA Ops:
  7.2 20.7 %copy-start = (s32[1,32]{1,0:T(1,128)S(1)}, s32[1,32]{1,0:T(1,128)}, u32[]{:S(2)}) copy-start(s32[1,32]{1,0:T(1,128)} %bmap.3) | copy-start | bytes 388
  7.2 114.9 %all-gather.2.cloned.1.call-start = ((), (), s32[]{:S(2)}) async-start(), calls=%async_computation | async-start | bytes 4456448 | tf_op jit(solution)/shard_map/all_gather | solution.py:455
  9.8 18.1 %collective-permute-start.3 = (f32[256,256]{1,0:T(8,128)}, f32[256,256]{1,0:T(8,128)S(1)}, u32[]{:S(2)}, u32[]{:S(2)}) collective-permute-start(f32[256,256]{1,0:T(8,128)} %get-tuple-element.70), channel_id=1, source_target_pairs={{3,68},{7,72},{11,76},{15,80},{19,84},{23,88},{27,92},{31,96},{35,... | collective-permute-start | bytes 786440 | tf_op jit(solution)/shard_map/ppermute | solution.py:27
  11.1 13.5 %collective-permute-start.1 = (f32[256,128]{1,0:T(8,128)}, f32[256,128]{1,0:T(8,128)S(1)}, u32[]{:S(2)}, u32[]{:S(2)}) collective-permute-start(f32[256,128]{1,0:T(8,128)} %get-tuple-element.50), channel_id=1, source_target_pairs={{0,68},{4,72},{8,76},{12,80},{16,84},{20,88},{24,92},{28,96},{32,1... | collective-permute-start | bytes 393224 | tf_op jit(solution)/shard_map/ppermute | solution.py:27
  16.9 10.9 %collective-permute-start.2 = (f32[128,256]{1,0:T(8,128)}, f32[128,256]{1,0:T(8,128)S(1)}, u32[]{:S(2)}, u32[]{:S(2)}) collective-permute-start(f32[128,256]{1,0:T(8,128)} %get-tuple-element.69), channel_id=1, source_target_pairs={{3,64},{7,68},{11,72},{15,76},{19,80},{23,84},{27,88},{31,92},{35,... | collective-permute-start | bytes 393224 | tf_op jit(solution)/shard_map/ppermute | solution.py:27
  18.2 6.3 %collective-permute-start = (f32[128,128]{1,0:T(8,128)}, f32[128,128]{1,0:T(8,128)S(1)}, u32[]{:S(2)}, u32[]{:S(2)}) collective-permute-start(f32[128,128]{1,0:T(8,128)} %get-tuple-element.49), channel_id=1, source_target_pairs={{0,64},{4,68},{8,72},{12,76},{16,80},{20,84},{24,88},{28,92},{32,9... | collective-permute-start | bytes 196616 | tf_op jit(solution)/shard_map/ppermute | solution.py:27
  28.7 18.6 %collective-permute-start.4 = (f32[128,512]{1,0:T(8,128)S(1)}, f32[128,512]{1,0:T(8,128)S(1)}, u32[]{:S(2)}, u32[]{:S(2)}) collective-permute-start(f32[128,512]{1,0:T(8,128)S(1)} %get-tuple-element.54.q1), channel_id=1, source_target_pairs={{0,1},{4,5},{8,9},{12,13},{16,17},{20,21},{24,25},{28,29},{32,33},... | collective-permute-start | bytes 786440 | tf_op jit(solution)/shard_map/ppermute | solution.py:27
  30.1 17.3 %collective-permute-start.5 = (f32[128,512]{1,0:T(8,128)S(1)}, f32[128,512]{1,0:T(8,128)S(1)}, u32[]{:S(2)}, u32[]{:S(2)}) collective-permute-start(f32[128,512]{1,0:T(8,128)S(1)} %get-tuple-element.55.q2), channel_id=1, source_target_pairs={{0,2},{4,6},{8,10},{12,14},{16,18},{20,22},{24,26},{28,30},{32,34}... | collective-permute-start | bytes 786440 | tf_op jit(solution)/shard_map/ppermute | solution.py:27
  31.4 23.9 %copy-start.15 = (f32[128,256]{1,0:T(8,128)S(1)}, f32[128,256]{1,0:T(8,128)}, u32[]{:S(2)}) copy-start(f32[128,256]{1,0:T(8,128)} %get-tuple-element.69) | copy-start | bytes 393220
  31.4 16.0 %collective-permute-start.6 = (f32[128,512]{1,0:T(8,128)S(1)}, f32[128,512]{1,0:T(8,128)S(1)}, u32[]{:S(2)}, u32[]{:S(2)}) collective-permute-start(f32[128,512]{1,0:T(8,128)S(1)} %get-tuple-element.56.q3), channel_id=1, source_target_pairs={{0,3},{4,7},{8,11},{12,15},{16,19},{20,23},{24,27},{28,31},{32,35}... | collective-permute-start | bytes 786440 | tf_op jit(solution)/shard_map/ppermute | solution.py:27
  32.8 14.5 %collective-permute-start.7 = (f32[128,1024]{1,0:T(8,128)}, f32[128,1024]{1,0:T(8,128)S(1)}, u32[]{:S(2)}, u32[]{:S(2)}) collective-permute-start(f32[128,1024]{1,0:T(8,128)} %get-tuple-element.59), channel_id=1, source_target_pairs={{0,64},{1,65},{2,66},{3,67},{4,68},{5,69},{6,70},{7,71},{8,72},{9,... | collective-permute-start | bytes 1572872 | tf_op jit(solution)/shard_map/ppermute | solution.py:27
  33.1 14.3 %collective-permute-start.8 = (f32[128,1024]{1,0:T(8,128)}, f32[128,1024]{1,0:T(8,128)S(1)}, u32[]{:S(2)}, u32[]{:S(2)}) collective-permute-start(f32[128,1024]{1,0:T(8,128)} %get-tuple-element.60), channel_id=1, source_target_pairs={{0,4},{1,5},{2,6},{3,7},{4,8},{5,9},{6,10},{7,11},{8,12},{9,13},{1... | collective-permute-start | bytes 1572872 | tf_op jit(solution)/shard_map/ppermute | solution.py:27
  47.4 23.4 %copy-start.3 = (f32[128,1024]{1,0:T(8,128)}, f32[128,1024]{1,0:T(8,128)S(1)}, u32[]{:S(2)}) copy-start(f32[128,1024]{1,0:T(8,128)S(1)} %collective-permute-done.7.own) | copy-start | bytes 1572868
  47.5 31.0 %copy-start.1 = (f32[128,512]{1,0:T(8,128)}, f32[128,512]{1,0:T(8,128)S(1)}, u32[]{:S(2)}) copy-start(f32[128,512]{1,0:T(8,128)S(1)} %add_select_fusion.a0) | copy-start | bytes 786436
  47.5 23.3 %collective-permute-start.9 = (f32[128,512]{1,0:T(8,128)S(1)}, f32[128,512]{1,0:T(8,128)S(1)}, u32[]{:S(2)}, u32[]{:S(2)}) collective-permute-start(f32[128,512]{1,0:T(8,128)S(1)} %add_select_fusion.a0), channel_id=1, source_target_pairs={{0,0},{1,4},{2,8},{3,12},{4,16},{5,20},{6,24},{7,28},{8,32},{9,36}... | collective-permute-start | bytes 786440 | tf_op jit(solution)/shard_map/ppermute | solution.py:27
  50.8 20.6 %collective-permute-start.10 = (f32[128,1024]{1,0:T(8,128)S(1)}, f32[128,1024]{1,0:T(8,128)S(1)}, u32[]{:S(2)}, u32[]{:S(2)}) collective-permute-start(f32[128,1024]{1,0:T(8,128)S(1)} %collective-permute-done.7.own), channel_id=1, source_target_pairs={{0,4},{1,5},{2,6},{3,7},{4,8},{5,9},{6,10},{7,11},{8,12},{9,13},{1... | collective-permute-start | bytes 1572872 | tf_op jit(solution)/shard_map/ppermute | solution.py:27
  55.3 15.5 %collective-permute-start.12 = (f32[128,256]{1,0:T(8,128)S(1)}, f32[128,256]{1,0:T(8,128)S(1)}, u32[]{:S(2)}, u32[]{:S(2)}) collective-permute-start(f32[128,256]{1,0:T(8,128)S(1)} %copy-done.15), channel_id=1, source_target_pairs={{0,1},{1,2},{2,3},{3,0},{4,5},{5,6},{6,7},{7,4},{8,9},{9,10},{10,1... | collective-permute-start | bytes 393224 | tf_op jit(solution)/shard_map/ppermute | solution.py:27
  57.2 13.6 %collective-permute-start.13 = (f32[256,256]{1,0:T(8,128)}, f32[256,256]{1,0:T(8,128)}, u32[]{:S(2)}, u32[]{:S(2)}) collective-permute-start(f32[256,256]{1,0:T(8,128)} %get-tuple-element.70), channel_id=1, source_target_pairs={{0,5},{1,6},{2,7},{3,4},{4,9},{5,10},{6,11},{7,8},{8,13},{9,14},{1... | collective-permute-start | bytes 786440 | tf_op jit(solution)/shard_map/ppermute | solution.py:27
  58.2 13.2 %collective-permute-start.11 = (f32[128,1024]{1,0:T(8,128)S(1)}, f32[128,1024]{1,0:T(8,128)S(1)}, u32[]{:S(2)}, u32[]{:S(2)}) collective-permute-start(f32[128,1024]{1,0:T(8,128)S(1)} %collective-permute-done.8), channel_id=1, source_target_pairs={{0,64},{1,65},{2,66},{3,67},{4,68},{5,69},{6,70},{7,71},{8,72},{9,... | collective-permute-start | bytes 1572872 | tf_op jit(solution)/shard_map/ppermute | solution.py:27
  70.8 0.7 copy-start.10
  71.4 50.7 %copy-start.5 = (f32[128,1024]{1,0:T(8,128)}, f32[128,1024]{1,0:T(8,128)S(1)}, u32[]{:S(2)}) copy-start(f32[128,1024]{1,0:T(8,128)S(1)} %collective-permute-done.11.prev1) | copy-start | bytes 1572868
  71.4 50.7 %copy-start.4 = (f32[128,1024]{1,0:T(8,128)}, f32[128,1024]{1,0:T(8,128)S(1)}, u32[]{:S(2)}) copy-start(f32[128,1024]{1,0:T(8,128)S(1)} %collective-permute-done.10.prev0) | copy-start | bytes 1572868
  71.5 2.0 %collective-permute-start.14 = (f32[320,128]{1,0:T(8,128)S(1)}, f32[320,128]{1,0:T(8,128)S(1)}, u32[]{:S(2)}, u32[]{:S(2)}) collective-permute-start(f32[320,128]{1,0:T(8,128)S(1)} %get-tuple-element.81), channel_id=1, source_target_pairs={{0,1},{64,65},{128,129},{192,193}} | collective-permute-start | bytes 491528 | tf_op jit(solution)/shard_map/ppermute | solution.py:27
  72.2 1.4 collective-permute-start.15
  72.9 0.7 collective-permute-start.16
  73.6 4.9 %collective-permute-start.18 = (f32[320,128]{1,0:T(8,128)S(1)}, f32[320,128]{1,0:T(8,128)S(1)}, u32[]{:S(2)}, u32[]{:S(2)}) collective-permute-start(f32[320,128]{1,0:T(8,128)S(1)} %add_select_fusion.3), channel_id=1, source_target_pairs={{0,48},{1,49},{2,50},{3,51},{64,112},{65,113},{66,114},{67,115},{1... | collective-permute-start | bytes 491528 | tf_op jit(solution)/shard_map/ppermute | solution.py:27
  74.3 4.2 %collective-permute-start.17 = (f32[320,128]{1,0:T(8,128)S(1)}, f32[320,128]{1,0:T(8,128)S(1)}, u32[]{:S(2)}, u32[]{:S(2)}) collective-permute-start(f32[320,128]{1,0:T(8,128)S(1)} %add_select_fusion.3), channel_id=1, source_target_pairs={{0,24},{1,25},{2,26},{3,27},{64,88},{65,89},{66,90},{67,91},{128,1... | collective-permute-start | bytes 491528 | tf_op jit(solution)/shard_map/ppermute | solution.py:27
  75.0 8.4 %collective-permute-start.21 = (f32[128,512]{1,0:T(8,128)S(1)}, f32[128,512]{1,0:T(8,128)S(1)}, u32[]{:S(2)}, u32[]{:S(2)}) collective-permute-start(f32[128,512]{1,0:T(8,128)S(1)} %add_select_fusion.a0), channel_id=1, source_target_pairs={{0,3},{1,0},{2,1},{3,2},{4,7},{5,4},{6,5},{7,6},{8,11},{9,8},{10,9... | collective-permute-start | bytes 786440 | tf_op jit(solution)/shard_map/ppermute | solution.py:27
  76.9 6.8 %collective-permute-start.20 = (f32[128,512]{1,0:T(8,128)S(1)}, f32[128,512]{1,0:T(8,128)S(1)}, u32[]{:S(2)}, u32[]{:S(2)}) collective-permute-start(f32[128,512]{1,0:T(8,128)S(1)} %add_select_fusion.a0), channel_id=1, source_target_pairs={{0,2},{1,3},{2,0},{3,1},{4,6},{5,7},{6,4},{7,5},{8,10},{9,11},{10,... | collective-permute-start | bytes 786440 | tf_op jit(solution)/shard_map/ppermute | solution.py:27
  78.5 8.0 %collective-permute-start.19 = (f32[128,512]{1,0:T(8,128)S(1)}, f32[128,512]{1,0:T(8,128)S(1)}, u32[]{:S(2)}, u32[]{:S(2)}) collective-permute-start(f32[128,512]{1,0:T(8,128)S(1)} %add_select_fusion.a0), channel_id=1, source_target_pairs={{0,1},{1,2},{2,3},{3,0},{4,5},{5,6},{6,7},{7,4},{8,9},{9,10},{10,1... | collective-permute-start | bytes 786440 | tf_op jit(solution)/shard_map/ppermute | solution.py:27
  83.4 38.7 %copy-start.6 = (f32[128,512]{1,0:T(8,128)}, f32[128,512]{1,0:T(8,128)S(1)}, u32[]{:S(2)}) copy-start(f32[128,512]{1,0:T(8,128)S(1)} %collective-permute-done.21.a3) | copy-start | bytes 786436
  83.7 38.3 %copy-start.7 = (f32[128,512]{1,0:T(8,128)}, f32[128,512]{1,0:T(8,128)S(1)}, u32[]{:S(2)}) copy-start(f32[128,512]{1,0:T(8,128)S(1)} %collective-permute-done.20.a2) | copy-start | bytes 786436
  86.5 35.7 %copy-start.8 = (f32[128,512]{1,0:T(8,128)}, f32[128,512]{1,0:T(8,128)S(1)}, u32[]{:S(2)}) copy-start(f32[128,512]{1,0:T(8,128)S(1)} %collective-permute-done.19.a1) | copy-start | bytes 786436
  86.5 1.4 collective-permute-start.23
  87.1 0.7 collective-permute-start.22
  87.9 21.9 %collective-permute-start.24 = (f32[320,128]{1,0:T(8,128)S(1)}, f32[320,128]{1,0:T(8,128)S(1)}, u32[]{:S(2)}, u32[]{:S(2)}) collective-permute-start(f32[320,128]{1,0:T(8,128)S(1)} %add_select_fusion.1), channel_id=1, source_target_pairs={{0,4},{1,5},{2,6},{3,7},{8,12},{9,13},{10,14},{11,15},{16,20},{17,... | collective-permute-start | bytes 491528 | tf_op jit(solution)/shard_map/ppermute | solution.py:27
  89.2 27.4 %collective-permute-start.29 = (f32[256,256]{1,0:T(8,128)}, f32[256,256]{1,0:T(8,128)S(1)}, u32[]{:S(2)}, u32[]{:S(2)}) collective-permute-start(f32[256,256]{1,0:T(8,128)} %collective-permute-done.13), channel_id=1, source_target_pairs={{0,64},{1,65},{2,66},{3,67},{4,68},{5,69},{6,70},{7,71},{8,72},{9,... | collective-permute-start | bytes 786440 | tf_op jit(solution)/shard_map/ppermute | solution.py:27
  109.8 12.3 %copy-start.2 = (f32[320,128]{1,0:T(8,128)}, f32[320,128]{1,0:T(8,128)S(1)}, u32[]{:S(2)}) copy-start(f32[320,128]{1,0:T(8,128)S(1)} %broadcast_select_fusion.l0) | copy-start | bytes 491524
  109.8 6.8 %collective-permute-start.27 = (f32[320,128]{1,0:T(8,128)S(1)}, f32[320,128]{1,0:T(8,128)S(1)}, u32[]{:S(2)}, u32[]{:S(2)}) collective-permute-start(f32[320,128]{1,0:T(8,128)S(1)} %broadcast_select_fusion.l0), channel_id=1, source_target_pairs={{0,3},{1,0},{2,1},{3,2},{4,7},{5,4},{6,5},{7,6},{8,11},{9,8},{10,9... | collective-permute-start | bytes 491528 | tf_op jit(solution)/shard_map/ppermute | solution.py:27
  111.6 6.3 %collective-permute-start.26 = (f32[320,128]{1,0:T(8,128)S(1)}, f32[320,128]{1,0:T(8,128)S(1)}, u32[]{:S(2)}, u32[]{:S(2)}) collective-permute-start(f32[320,128]{1,0:T(8,128)S(1)} %broadcast_select_fusion.l0), channel_id=1, source_target_pairs={{0,2},{1,3},{2,0},{3,1},{4,6},{5,7},{6,4},{7,5},{8,10},{9,11},{10,... | collective-permute-start | bytes 491528 | tf_op jit(solution)/shard_map/ppermute | solution.py:27
  111.6 10.5 %collective-permute-start.25 = (f32[320,128]{1,0:T(8,128)S(1)}, f32[320,128]{1,0:T(8,128)S(1)}, u32[]{:S(2)}, u32[]{:S(2)}) collective-permute-start(f32[320,128]{1,0:T(8,128)S(1)} %broadcast_select_fusion.l0), channel_id=1, source_target_pairs={{0,1},{1,2},{2,3},{3,0},{4,5},{5,6},{6,7},{7,4},{8,9},{9,10},{10,1... | collective-permute-start | bytes 491528 | tf_op jit(solution)/shard_map/ppermute | solution.py:27
  112.3 4.3 %collective-permute-start.28 = (f32[128,256]{1,0:T(8,128)S(1)}, f32[128,256]{1,0:T(8,128)S(1)}, u32[]{:S(2)}, u32[]{:S(2)}) collective-permute-start(f32[128,256]{1,0:T(8,128)S(1)} %collective-permute-done.12), channel_id=1, source_target_pairs={{0,64},{1,65},{2,66},{3,67},{4,68},{5,69},{6,70},{7,71},{8,72},{9,... | collective-permute-start | bytes 393224 | tf_op jit(solution)/shard_map/ppermute | solution.py:27
  116.6 5.5 %copy-start.14 = (f32[128,256]{1,0:T(8,128)}, f32[128,256]{1,0:T(8,128)S(1)}, u32[]{:S(2)}) copy-start(f32[128,256]{1,0:T(8,128)S(1)} %collective-permute-done.28.edge0) | copy-start | bytes 393220
  116.6 5.5 %copy-start.9 = (f32[256,256]{1,0:T(8,128)}, f32[256,256]{1,0:T(8,128)S(1)}, u32[]{:S(2)}) copy-start(f32[256,256]{1,0:T(8,128)S(1)} %collective-permute-done.29.edge1) | copy-start | bytes 786436
  116.6 5.5 %copy-start.11 = (f32[320,128]{1,0:T(8,128)}, f32[320,128]{1,0:T(8,128)S(1)}, u32[]{:S(2)}) copy-start(f32[320,128]{1,0:T(8,128)S(1)} %collective-permute-done.27.l3) | copy-start | bytes 491524
  117.9 4.3 %copy-start.12 = (f32[320,128]{1,0:T(8,128)}, f32[320,128]{1,0:T(8,128)S(1)}, u32[]{:S(2)}) copy-start(f32[320,128]{1,0:T(8,128)S(1)} %collective-permute-done.26.l2) | copy-start | bytes 491524
  122.1 0.7 copy-start.13
Sparse Core Ops, SparseCore 0:
  71.7 39.2 all-gather.1

commit v3 on v2

--- a/solution.py
+++ b/solution.py
@@ -320,7 +320,7 @@
                 (own, (upper, right)),
                 (prev0, (middle, right)),
                 (prev1, (lower, right)),
-                (edge0, (upper, left)),
+                (edge0.at[upper, :], (upper, left)),
                 (edge1, (rest, left)),
             ]
         )
@@ -428,7 +428,7 @@
     def across(x):
         return permute(x, lambda f, r, c: (f ^ 1, r, c))
 
-    top, bottom, e0, e1, _ = lax.optimization_barrier((top, bottom, e0, e1, quarter[0]))
+    top, bottom, _ = lax.optimization_barrier((top, bottom, quarter[0]))
     own = across(top)
     prev1 = permute(bottom, lambda f, r, c: (f, (r + 1) % ROWS, c))
 
@@ -437,21 +437,22 @@
     ]
 
     half = first_call(quarter)
-    *got, own, prev1, e0, e1, _ = lax.optimization_barrier((*got, own, prev1, e0, e1, half[0]))
+    *got, own, prev1, _ = lax.optimization_barrier((*got, own, prev1, half[0]))
     prev1 = across(prev1)
-    prev0 = permute(own, lambda f, r, c: (f, (r + 1) % ROWS, c))
-    edge0 = permute(e0, lambda f, r, c: (f, r, (c + 1) % COLS))
-    edge1 = permute(e1, lambda f, r, c: (f, (r + 1) % ROWS, (c + 1) % COLS))
     mine = jnp.where(c == 0, quarter[0], got[0] + got[1] + got[2])
 
     piece = permute(mine, lambda f, r, c: (f, 4 * (r % 4) + c, r // 4))
+
+    a_parts = [permute(mine, lambda f, r, c, s=s: (f, r, (c + s) % COLS)) for s in (1, 2, 3)]
 
     *half, _, _ = lax.optimization_barrier((*half, mine, own))
     part = second_call(*half)
-    piece, prev0, prev1, edge0, edge1, *part = lax.optimization_barrier(
-        (piece, prev0, prev1, edge0, edge1, *part)
+    piece, prev1, own, e1, *part = lax.optimization_barrier(
+        (piece, prev1, own, e1, *part, *a_parts)
     )
-    edge0, edge1 = across(edge0), across(edge1)
+    part, a_parts = part[:4], [mine, *part[4:]]
+    prev0 = permute(own, lambda f, r, c: (f, (r + 1) % ROWS, c))
+    edge = permute(e1, lambda f, r, c: (f, r, (c + 1) % COLS))
     a_col = lax.all_gather(piece, "row", axis=0, tiled=True)
 
     got = [
@@ -459,18 +460,16 @@
         for q in (1, 2, 3)
     ]
     d = jnp.where(c == 0, part[0], got[0] + got[1] + got[2])
-
-    m = after(mine, part[0])
-    a_parts = [permute(m, lambda f, r, c, s=s: (f, r, (c + s) % COLS)) for s in (1, 2, 3)]
-
     d1 = permute(d, lambda f, r, c: (f, 6, c) if r == 0 else None)
     d2 = permute(d, lambda f, r, c: (f, 12, c) if r == 0 else None)
     d = jnp.where(row == 0, d, d1 + d2)
-    d, *a_parts = lax.optimization_barrier((d, *a_parts))
-    a_parts = [mine, *a_parts]
+    d, prev0, edge = lax.optimization_barrier((d, prev0, edge))
+    edge0 = across(edge)
     d1 = permute(d, lambda f, r, c: (f, (r + 2) % ROWS, c) if r in (0, 6, 12) else None)
     d2 = permute(d, lambda f, r, c: (f, r - 2, c) if r in (6, 12) else None)
     d = jnp.where((row == 0) | (row == 6) | (row == 12), d, d1 + d2)
+    d, edge0 = lax.optimization_barrier((d, edge0))
+    edge1 = permute(edge0, lambda f, r, c: (f, (r + 1) % ROWS, c))
     d1 = permute(d, lambda f, r, c: (f, r + 1, c) if r % 2 == 0 else None)
     d = jnp.where(row % 2 == 0, d, d1)
     l_parts = [d] + [permute(d, lambda f, r, c, s=s: (f, r, (c + s) % COLS)) for s in (1, 2, 3)]

time: 142 us -> 134 us (0.944)
  waiting for transfers between devices: 42 us -> 31.6 us
  starting transfers between devices: 42.1 us -> 44.8 us
    ppermute x30 -> x29, waiting for transfers between devices: 42 us -> 28.9 us  [permute(): return lax.ppermute(x, AXES, pairs)]
    all_gather x1, waiting for transfers between devices: 0.01 us -> 2.65 us  [body(): a_col = lax.all_gather(piece, 'row', axis=0, tiled=True)]
    ppermute x30 -> x29, starting transfers between devices: 42.1 us -> 44.7 us  [permute(): return lax.ppermute(x, AXES, pairs)]
  transfers between devices with their start and end apart: 31 -> 30, of which waited for: 10 -> 10; matrix products, arithmetic and copies ran while one was open for 1% -> 1% of each run, Pallas kernels for 17% -> 18%
where the time goes in v3:
time: 134 us
  starting transfers between devices  44.8 us (33%)
  Pallas kernels  39.8 us (30%)
  waiting for transfers between devices  31.6 us (24%)
  between operations  15.1 us (11%)
  local copies, waits for them, and re-layouts  2.05 us (2%)
    ppermute x29, starting transfers between devices, permute(): return lax.ppermute(x, AXES, pairs)  44.7 us
    ppermute x29, waiting for transfers between devices, permute(): return lax.ppermute(x, AXES, pairs)  28.9 us
    pallas_call x1, Pallas kernels, first_call(): pl.pallas_call(first_kernel, grid=(1,), in_specs=[whole((128, 512))] * 4,...  12.4 us
    pallas_call x1, Pallas kernels, second_call(): pl.pallas_call(second_kernel, grid=(1,), in_specs=[whole(HALF)] * 3, out_...  12.3 us
    pallas_call x1, Pallas kernels, update_call(): pl.pallas_call(update_kernel, grid=(1,), in_specs=[smem(), smem()] + [who...  11.7 us
  transfers between devices with their start and end apart: 30, of which 10 were waited for; matrix products, arithmetic and copies ran while one was open for 1% of the time, Pallas kernels for 18%

profile of v3, /device:TPU:1, one launch (start us, length us, event | category | flops | bytes accessed | tf_op | source)
XLA Modules:
  0.0 133.6 jit_solution(9459829426294921254)
XLA Ops:
  7.2 0.0 copy-start
  7.2 0.0 all-gather.2.cloned.1.call-start
  7.2 2.6 %pack.1 = (f32[128,128]{1,0:T(8,128)}, f32[256,128]{1,0:T(8,128)}, f32[128,256]{1,0:T(8,128)}, f32[256,256]{1,0:T(8,128)}, f32[128,1024]{1,0:T(8,128)}, /*index=5*/f32[128,1024]{1,0:T(8,128)}) custom-call(f32[256,1024]{1,0:T(8,128)} %bitcast.4, f32[256,1024]{1,0:T(8,128)} %bitcast.5, f32[256,1024]{1,0:T(8,128)} %bitcast.6), custom_call_target="tpu_custom_call" | custom-call | tf_op jit(solution)/shard_map/pack/pallas_call | solution.py:72
  9.8 1.3 collective-permute-start.3
  11.1 5.9 %collective-permute-start.1 = (f32[256,128]{1,0:T(8,128)}, f32[256,128]{1,0:T(8,128)S(1)}, u32[]{:S(2)}, u32[]{:S(2)}) collective-permute-start(f32[256,128]{1,0:T(8,128)} %get-tuple-element.48), channel_id=1, source_target_pairs={{0,68},{4,72},{8,76},{12,80},{16,84},{20,88},{24,92},{28,96},{32,1... | collective-permute-start | bytes 393224 | tf_op jit(solution)/shard_map/ppermute | solution.py:27
  16.9 1.3 collective-permute-start.2
  18.2 2.2 %collective-permute-start = (f32[128,128]{1,0:T(8,128)}, f32[128,128]{1,0:T(8,128)S(1)}, u32[]{:S(2)}, u32[]{:S(2)}) collective-permute-start(f32[128,128]{1,0:T(8,128)} %get-tuple-element.47), channel_id=1, source_target_pairs={{0,64},{4,68},{8,72},{12,76},{16,80},{20,84},{24,88},{28,92},{32,9... | collective-permute-start | bytes 196616 | tf_op jit(solution)/shard_map/ppermute | solution.py:27
  21.1 1.3 slice.4.front
  22.4 2.2 %collective-permute-done.ea = f32[128,128]{1,0:T(8,128)S(1)} collective-permute-done((f32[128,128]{1,0:T(8,128)}, f32[128,128]{1,0:T(8,128)S(1)}, u32[]{:S(2)}, u32[]{:S(2)}) %collective-permute-start) | collective-permute-done | bytes 65568 | tf_op jit(solution)/shard_map/ppermute | solution.py:27
  24.6 0.0 collective-permute-done.1.eb
  24.6 3.3 %collective-permute-done.2.ed = f32[128,256]{1,0:T(8,128)S(1)} collective-permute-done((f32[128,256]{1,0:T(8,128)}, f32[128,256]{1,0:T(8,128)S(1)}, u32[]{:S(2)}, u32[]{:S(2)}) %collective-permute-start.2) | collective-permute-done | bytes 131104 | tf_op jit(solution)/shard_map/ppermute | solution.py:27
  27.9 0.0 collective-permute-done.3.ee
  27.9 0.9 panel.1
  28.8 1.3 collective-permute-start.4
  30.1 1.3 collective-permute-start.5
  31.4 1.3 collective-permute-start.6
  32.7 0.3 collective-permute-start.7
  33.0 1.9 %collective-permute-start.8 = (f32[128,1024]{1,0:T(8,128)}, f32[128,1024]{1,0:T(8,128)S(1)}, u32[]{:S(2)}, u32[]{:S(2)}) collective-permute-start(f32[128,1024]{1,0:T(8,128)} %get-tuple-element.58), channel_id=1, source_target_pairs={{0,4},{1,5},{2,6},{3,7},{4,8},{5,9},{6,10},{7,11},{8,12},{9,13},{1... | collective-permute-start | bytes 1572872 | tf_op jit(solution)/shard_map/ppermute | solution.py:27
  34.8 12.4 %first.1 = (f32[256,256]{1,0:T(8,128)S(1)}, f32[256,256]{1,0:T(8,128)S(1)}, f32[256,256]{1,0:T(8,128)S(1)}) custom-call(f32[128,512]{1,0:T(8,128)S(1)} %get-tuple-element.51.q0, f32[128,512]{1,0:T(8,128)S(1)} %get-tuple-element.52.q1, f32[128,512]{1,0:T(8,128)S(1)} %get-tuple-element.53.q2, f32[128,512]{1,0:T(8,128)S(1)} %get-tuple-element.54.q3), custom_call_target="tpu_custom_call" | custom-call | flops 10000000000 | bytes 4194304 | tf_op jit(solution)/shard_map/first/pallas_call | solution.py:221
  47.2 0.0 collective-permute-done.4
  47.2 0.0 collective-permute-done.5
  47.2 0.0 collective-permute-done.6
  47.2 0.0 collective-permute-done.7.own
  47.2 0.0 collective-permute-done.8
  47.3 0.1 add_select_fusion.a0
  47.4 0.1 collective-permute-start.13
  47.5 0.1 collective-permute-start.12
  47.6 1.4 %collective-permute-start.11 = (f32[128,512]{1,0:T(8,128)S(1)}, f32[128,512]{1,0:T(8,128)S(1)}, u32[]{:S(2)}, u32[]{:S(2)}) collective-permute-start(f32[128,512]{1,0:T(8,128)S(1)} %add_select_fusion.a0), channel_id=1, source_target_pairs={{0,1},{1,2},{2,3},{3,0},{4,5},{5,6},{6,7},{7,4},{8,9},{9,10},{10,1... | collective-permute-start | bytes 786440 | tf_op jit(solution)/shard_map/ppermute | solution.py:27
  48.9 3.8 %collective-permute-start.9 = (f32[128,512]{1,0:T(8,128)S(1)}, f32[128,512]{1,0:T(8,128)S(1)}, u32[]{:S(2)}, u32[]{:S(2)}) collective-permute-start(f32[128,512]{1,0:T(8,128)S(1)} %add_select_fusion.a0), channel_id=1, source_target_pairs={{0,0},{1,4},{2,8},{3,12},{4,16},{5,20},{6,24},{7,28},{8,32},{9,36}... | collective-permute-start | bytes 786440 | tf_op jit(solution)/shard_map/ppermute | solution.py:27
  52.8 1.0 collective-permute-start.10
  53.7 12.3 %second.1 = (f32[320,128]{1,0:T(8,128)S(1)}, f32[320,128]{1,0:T(8,128)S(1)}, f32[320,128]{1,0:T(8,128)S(1)}, f32[320,128]{1,0:T(8,128)S(1)}) custom-call(f32[256,256]{1,0:T(8,128)S(1)} %get-tuple-element.67.inv, f32[256,256]{1,0:T(8,128)S(1)} %get-tuple-element.68.below, f32[256,256]{1,0:T(8,128)S(1)} %get-tuple-element.69.rest), custom_call_target="tpu_custom_call" | custom-call | flops 10000000000 | bytes 4194304 | tf_op jit(solution)/shard_map/second/pallas_call | solution.py:261
  66.1 0.0 collective-permute-done.13.a3
  66.1 0.0 collective-permute-done.12.a2
  66.1 2.7 %collective-permute-done.9 = f32[128,512]{1,0:T(8,128)S(1)} collective-permute-done((f32[128,512]{1,0:T(8,128)S(1)}, f32[128,512]{1,0:T(8,128)S(1)}, u32[]{:S(2)}, u32[]{:S(2)}) %collective-permute-start.9) | collective-permute-done | bytes 262176 | tf_op jit(solution)/shard_map/ppermute | solution.py:27
  68.8 0.0 collective-permute-done.10.prev1
  68.8 0.7 copy-done.11
  69.5 0.0 all-gather.2.cloned.1.call-update
  69.6 0.7 collective-permute-start.14
  70.2 0.7 collective-permute-start.15
  70.9 0.7 collective-permute-start.16
  71.6 2.3 %collective-permute-start.19 = (f32[128,1024]{1,0:T(8,128)S(1)}, f32[128,1024]{1,0:T(8,128)S(1)}, u32[]{:S(2)}, u32[]{:S(2)}) collective-permute-start(f32[128,1024]{1,0:T(8,128)S(1)} %collective-permute-done.7.own), channel_id=1, source_target_pairs={{0,4},{1,5},{2,6},{3,7},{4,8},{5,9},{6,10},{7,11},{8,12},{9,13},{1... | collective-permute-start | bytes 1572872 | tf_op jit(solution)/shard_map/ppermute | solution.py:27
  73.9 0.0 collective-permute-done.14
  73.9 0.0 collective-permute-done.15
  74.0 0.0 collective-permute-done.16
  74.0 0.7 collective-permute-start.18
  74.7 0.7 collective-permute-start.17
  75.4 1.0 collective-permute-start.20
  76.4 0.0 collective-permute-done.17
  76.4 5.7 %collective-permute-done.20 = f32[256,256]{1,0:T(8,128)S(1)} collective-permute-done((f32[256,256]{1,0:T(8,128)S(1)}, f32[256,256]{1,0:T(8,128)S(1)}, u32[]{:S(2)}, u32[]{:S(2)}) %collective-permute-start.20) | collective-permute-done | bytes 262176 | tf_op jit(solution)/shard_map/ppermute | solution.py:27
  82.2 0.0 collective-permute-done.19.prev0
  82.2 0.7 collective-permute-start.22
  82.8 0.7 collective-permute-start.21
  83.5 1.0 collective-permute-start.23
  84.6 4.7 %collective-permute-done.23.edge0 = f32[256,256]{1,0:T(8,128)S(1)} collective-permute-done((f32[256,256]{1,0:T(8,128)S(1)}, f32[256,256]{1,0:T(8,128)S(1)}, u32[]{:S(2)}, u32[]{:S(2)}) %collective-permute-start.23) | collective-permute-done | bytes 262176 | tf_op jit(solution)/shard_map/ppermute | solution.py:27
  89.2 1.3 collective-permute-start.24
  90.5 8.5 %collective-permute-start.28 = (f32[256,256]{1,0:T(8,128)S(1)}, f32[256,256]{1,0:T(8,128)S(1)}, u32[]{:S(2)}, u32[]{:S(2)}) collective-permute-start(f32[256,256]{1,0:T(8,128)S(1)} %collective-permute-done.23.edge0), channel_id=1, source_target_pairs={{0,4},{1,5},{2,6},{3,7},{4,8},{5,9},{6,10},{7,11},{8,12},{9,13},{1... | collective-permute-start | bytes 786440 | tf_op jit(solution)/shard_map/ppermute | solution.py:27
  99.1 2.2 %collective-permute-start.27 = (f32[320,128]{1,0:T(8,128)S(1)}, f32[320,128]{1,0:T(8,128)S(1)}, u32[]{:S(2)}, u32[]{:S(2)}) collective-permute-start(f32[320,128]{1,0:T(8,128)S(1)} %broadcast_select_fusion.l0), channel_id=1, source_target_pairs={{0,3},{1,0},{2,1},{3,2},{4,7},{5,4},{6,5},{7,6},{8,11},{9,8},{10,9... | collective-permute-start | bytes 491528 | tf_op jit(solution)/shard_map/ppermute | solution.py:27
  101.3 0.7 collective-permute-start.25
  102.0 5.4 %collective-permute-done.28.edge1 = f32[256,256]{1,0:T(8,128)S(1)} collective-permute-done((f32[256,256]{1,0:T(8,128)S(1)}, f32[256,256]{1,0:T(8,128)S(1)}, u32[]{:S(2)}, u32[]{:S(2)}) %collective-permute-start.28) | collective-permute-done | bytes 262176 | tf_op jit(solution)/shard_map/ppermute | solution.py:27
  107.4 1.2 collective-permute-done.27.l3
  108.5 0.5 collective-permute-done.26.l2
  109.0 3.3 %collective-permute-done.25.l1 = f32[320,128]{1,0:T(8,128)S(1)} collective-permute-done((f32[320,128]{1,0:T(8,128)S(1)}, f32[320,128]{1,0:T(8,128)S(1)}, u32[]{:S(2)}, u32[]{:S(2)}) %collective-permute-start.25) | collective-permute-done | bytes 163872 | tf_op jit(solution)/shard_map/ppermute | solution.py:27
  112.2 2.7 %all-gather.2.cloned.1.call-done.a_col = f32[2048,512]{1,0:T(8,128)} async-done(((f32[128,512]{1,0:T(8,128)}), f32[2048,512]{1,0:T(8,128)}) %all-gather.2.cloned.1.call-update) | async-done | bytes 4194320 | tf_op jit(solution)/shard_map/all_gather | solution.py:456
  115.0 11.7 %update.1 = (f32[512,512]{1,0:T(8,128)}, f32[512,2048]{1,0:T(8,128)}) custom-call(s32[1,32]{1,0:T(1,128)} %bmap.3, s32[1]{0:T(128)S(6)} %copy.6.order, f32[320,128]{1,0:T(8,128)} %copy-done.2, f32[320,128]{1,0:T(8,128)} %copy-done.14, f32[320,128]{1,0:T(8,128)} %copy-done.13, f32[320,128]{1,0:T(8,128)} %copy-done.12, f32[128,512]{1,0:T(8,128)} %copy-done.1, ...), custom_call_target="tpu_custom_call" | custom-call | tf_op jit(solution)/shard_map/update/pallas_call | solution.py:378
  (40 shorter events, 0.2 us)
Async XLA Ops:
  7.2 20.7 %copy-start = (s32[1,32]{1,0:T(1,128)S(1)}, s32[1,32]{1,0:T(1,128)}, u32[]{:S(2)}) copy-start(s32[1,32]{1,0:T(1,128)} %bmap.3) | copy-start | bytes 388
  7.2 107.7 %all-gather.2.cloned.1.call-start = ((), (), s32[]{:S(2)}) async-start(), calls=%async_computation | async-start | bytes 4456448 | tf_op jit(solution)/shard_map/all_gather | solution.py:456
  9.8 18.1 %collective-permute-start.3 = (f32[256,256]{1,0:T(8,128)}, f32[256,256]{1,0:T(8,128)S(1)}, u32[]{:S(2)}, u32[]{:S(2)}) collective-permute-start(f32[256,256]{1,0:T(8,128)} %get-tuple-element.79), channel_id=1, source_target_pairs={{3,68},{7,72},{11,76},{15,80},{19,84},{23,88},{27,92},{31,96},{35,... | collective-permute-start | bytes 786440 | tf_op jit(solution)/shard_map/ppermute | solution.py:27
  11.1 13.5 %collective-permute-start.1 = (f32[256,128]{1,0:T(8,128)}, f32[256,128]{1,0:T(8,128)S(1)}, u32[]{:S(2)}, u32[]{:S(2)}) collective-permute-start(f32[256,128]{1,0:T(8,128)} %get-tuple-element.48), channel_id=1, source_target_pairs={{0,68},{4,72},{8,76},{12,80},{16,84},{20,88},{24,92},{28,96},{32,1... | collective-permute-start | bytes 393224 | tf_op jit(solution)/shard_map/ppermute | solution.py:27
  16.9 10.9 %collective-permute-start.2 = (f32[128,256]{1,0:T(8,128)}, f32[128,256]{1,0:T(8,128)S(1)}, u32[]{:S(2)}, u32[]{:S(2)}) collective-permute-start(f32[128,256]{1,0:T(8,128)} %get-tuple-element.49), channel_id=1, source_target_pairs={{3,64},{7,68},{11,72},{15,76},{19,80},{23,84},{27,88},{31,92},{35,... | collective-permute-start | bytes 393224 | tf_op jit(solution)/shard_map/ppermute | solution.py:27
  18.2 6.3 %collective-permute-start = (f32[128,128]{1,0:T(8,128)}, f32[128,128]{1,0:T(8,128)S(1)}, u32[]{:S(2)}, u32[]{:S(2)}) collective-permute-start(f32[128,128]{1,0:T(8,128)} %get-tuple-element.47), channel_id=1, source_target_pairs={{0,64},{4,68},{8,72},{12,76},{16,80},{20,84},{24,88},{28,92},{32,9... | collective-permute-start | bytes 196616 | tf_op jit(solution)/shard_map/ppermute | solution.py:27
  28.8 18.4 %collective-permute-start.4 = (f32[128,512]{1,0:T(8,128)S(1)}, f32[128,512]{1,0:T(8,128)S(1)}, u32[]{:S(2)}, u32[]{:S(2)}) collective-permute-start(f32[128,512]{1,0:T(8,128)S(1)} %get-tuple-element.52.q1), channel_id=1, source_target_pairs={{0,1},{4,5},{8,9},{12,13},{16,17},{20,21},{24,25},{28,29},{32,33},... | collective-permute-start | bytes 786440 | tf_op jit(solution)/shard_map/ppermute | solution.py:27
  30.1 17.1 %collective-permute-start.5 = (f32[128,512]{1,0:T(8,128)S(1)}, f32[128,512]{1,0:T(8,128)S(1)}, u32[]{:S(2)}, u32[]{:S(2)}) collective-permute-start(f32[128,512]{1,0:T(8,128)S(1)} %get-tuple-element.53.q2), channel_id=1, source_target_pairs={{0,2},{4,6},{8,10},{12,14},{16,18},{20,22},{24,26},{28,30},{32,34}... | collective-permute-start | bytes 786440 | tf_op jit(solution)/shard_map/ppermute | solution.py:27
  31.4 15.8 %collective-permute-start.6 = (f32[128,512]{1,0:T(8,128)S(1)}, f32[128,512]{1,0:T(8,128)S(1)}, u32[]{:S(2)}, u32[]{:S(2)}) collective-permute-start(f32[128,512]{1,0:T(8,128)S(1)} %get-tuple-element.54.q3), channel_id=1, source_target_pairs={{0,3},{4,7},{8,11},{12,15},{16,19},{20,23},{24,27},{28,31},{32,35}... | collective-permute-start | bytes 786440 | tf_op jit(solution)/shard_map/ppermute | solution.py:27
  32.7 14.5 %collective-permute-start.7 = (f32[128,1024]{1,0:T(8,128)}, f32[128,1024]{1,0:T(8,128)S(1)}, u32[]{:S(2)}, u32[]{:S(2)}) collective-permute-start(f32[128,1024]{1,0:T(8,128)} %get-tuple-element.57), channel_id=1, source_target_pairs={{0,64},{1,65},{2,66},{3,67},{4,68},{5,69},{6,70},{7,71},{8,72},{9,... | collective-permute-start | bytes 1572872 | tf_op jit(solution)/shard_map/ppermute | solution.py:27
  33.0 14.3 %collective-permute-start.8 = (f32[128,1024]{1,0:T(8,128)}, f32[128,1024]{1,0:T(8,128)S(1)}, u32[]{:S(2)}, u32[]{:S(2)}) collective-permute-start(f32[128,1024]{1,0:T(8,128)} %get-tuple-element.58), channel_id=1, source_target_pairs={{0,4},{1,5},{2,6},{3,7},{4,8},{5,9},{6,10},{7,11},{8,12},{9,13},{1... | collective-permute-start | bytes 1572872 | tf_op jit(solution)/shard_map/ppermute | solution.py:27
  47.2 24.4 %copy-start.3 = (f32[128,1024]{1,0:T(8,128)}, f32[128,1024]{1,0:T(8,128)S(1)}, u32[]{:S(2)}) copy-start(f32[128,1024]{1,0:T(8,128)S(1)} %collective-permute-done.7.own) | copy-start | bytes 1572868
  47.4 18.7 %copy-start.1 = (f32[128,512]{1,0:T(8,128)}, f32[128,512]{1,0:T(8,128)S(1)}, u32[]{:S(2)}) copy-start(f32[128,512]{1,0:T(8,128)S(1)} %add_select_fusion.a0) | copy-start | bytes 786436
  47.4 18.7 %collective-permute-start.13 = (f32[128,512]{1,0:T(8,128)S(1)}, f32[128,512]{1,0:T(8,128)S(1)}, u32[]{:S(2)}, u32[]{:S(2)}) collective-permute-start(f32[128,512]{1,0:T(8,128)S(1)} %add_select_fusion.a0), channel_id=1, source_target_pairs={{0,3},{1,0},{2,1},{3,2},{4,7},{5,4},{6,5},{7,6},{8,11},{9,8},{10,9... | collective-permute-start | bytes 786440 | tf_op jit(solution)/shard_map/ppermute | solution.py:27
  47.5 18.6 %collective-permute-start.12 = (f32[128,512]{1,0:T(8,128)S(1)}, f32[128,512]{1,0:T(8,128)S(1)}, u32[]{:S(2)}, u32[]{:S(2)}) collective-permute-start(f32[128,512]{1,0:T(8,128)S(1)} %add_select_fusion.a0), channel_id=1, source_target_pairs={{0,2},{1,3},{2,0},{3,1},{4,6},{5,7},{6,4},{7,5},{8,10},{9,11},{10,... | collective-permute-start | bytes 786440 | tf_op jit(solution)/shard_map/ppermute | solution.py:27
  47.6 18.5 %collective-permute-start.11 = (f32[128,512]{1,0:T(8,128)S(1)}, f32[128,512]{1,0:T(8,128)S(1)}, u32[]{:S(2)}, u32[]{:S(2)}) collective-permute-start(f32[128,512]{1,0:T(8,128)S(1)} %add_select_fusion.a0), channel_id=1, source_target_pairs={{0,1},{1,2},{2,3},{3,0},{4,5},{5,6},{6,7},{7,4},{8,9},{9,10},{10,1... | collective-permute-start | bytes 786440 | tf_op jit(solution)/shard_map/ppermute | solution.py:27
  48.9 19.9 %collective-permute-start.9 = (f32[128,512]{1,0:T(8,128)S(1)}, f32[128,512]{1,0:T(8,128)S(1)}, u32[]{:S(2)}, u32[]{:S(2)}) collective-permute-start(f32[128,512]{1,0:T(8,128)S(1)} %add_select_fusion.a0), channel_id=1, source_target_pairs={{0,0},{1,4},{2,8},{3,12},{4,16},{5,20},{6,24},{7,28},{8,32},{9,36}... | collective-permute-start | bytes 786440 | tf_op jit(solution)/shard_map/ppermute | solution.py:27
  52.8 22.6 %copy-start.15 = (f32[256,256]{1,0:T(8,128)S(1)}, f32[256,256]{1,0:T(8,128)}, u32[]{:S(2)}) copy-start(f32[256,256]{1,0:T(8,128)} %get-tuple-element.79) | copy-start | bytes 786436
  52.8 16.1 %collective-permute-start.10 = (f32[128,1024]{1,0:T(8,128)S(1)}, f32[128,1024]{1,0:T(8,128)S(1)}, u32[]{:S(2)}, u32[]{:S(2)}) collective-permute-start(f32[128,1024]{1,0:T(8,128)S(1)} %collective-permute-done.8), channel_id=1, source_target_pairs={{0,64},{1,65},{2,66},{3,67},{4,68},{5,69},{6,70},{7,71},{8,72},{9,... | collective-permute-start | bytes 1572872 | tf_op jit(solution)/shard_map/ppermute | solution.py:27
  66.1 48.8 %copy-start.6 = (f32[128,512]{1,0:T(8,128)}, f32[128,512]{1,0:T(8,128)S(1)}, u32[]{:S(2)}) copy-start(f32[128,512]{1,0:T(8,128)S(1)} %collective-permute-done.13.a3) | copy-start | bytes 786436
  66.1 48.8 %copy-start.7 = (f32[128,512]{1,0:T(8,128)}, f32[128,512]{1,0:T(8,128)S(1)}, u32[]{:S(2)}) copy-start(f32[128,512]{1,0:T(8,128)S(1)} %collective-permute-done.12.a2) | copy-start | bytes 786436
  66.1 48.8 %copy-start.8 = (f32[128,512]{1,0:T(8,128)}, f32[128,512]{1,0:T(8,128)S(1)}, u32[]{:S(2)}) copy-start(f32[128,512]{1,0:T(8,128)S(1)} %collective-permute-done.11.a1) | copy-start | bytes 786436
  68.8 0.7 copy-start.11
  68.8 46.1 %copy-start.4 = (f32[128,1024]{1,0:T(8,128)}, f32[128,1024]{1,0:T(8,128)S(1)}, u32[]{:S(2)}) copy-start(f32[128,1024]{1,0:T(8,128)S(1)} %collective-permute-done.10.prev1) | copy-start | bytes 1572868
  69.6 4.4 %collective-permute-start.14 = (f32[320,128]{1,0:T(8,128)S(1)}, f32[320,128]{1,0:T(8,128)S(1)}, u32[]{:S(2)}, u32[]{:S(2)}) collective-permute-start(f32[320,128]{1,0:T(8,128)S(1)} %get-tuple-element.75), channel_id=1, source_target_pairs={{0,1},{64,65},{128,129},{192,193}} | collective-permute-start | bytes 491528 | tf_op jit(solution)/shard_map/ppermute | solution.py:27
  70.2 3.7 %collective-permute-start.15 = (f32[320,128]{1,0:T(8,128)S(1)}, f32[320,128]{1,0:T(8,128)S(1)}, u32[]{:S(2)}, u32[]{:S(2)}) collective-permute-start(f32[320,128]{1,0:T(8,128)S(1)} %get-tuple-element.76), channel_id=1, source_target_pairs={{0,2},{64,66},{128,130},{192,194}} | collective-permute-start | bytes 491528 | tf_op jit(solution)/shard_map/ppermute | solution.py:27
  70.9 3.0 %collective-permute-start.16 = (f32[320,128]{1,0:T(8,128)S(1)}, f32[320,128]{1,0:T(8,128)S(1)}, u32[]{:S(2)}, u32[]{:S(2)}) collective-permute-start(f32[320,128]{1,0:T(8,128)S(1)} %get-tuple-element.77), channel_id=1, source_target_pairs={{0,3},{64,67},{128,131},{192,195}} | collective-permute-start | bytes 491528 | tf_op jit(solution)/shard_map/ppermute | solution.py:27
  71.6 10.6 %collective-permute-start.19 = (f32[128,1024]{1,0:T(8,128)S(1)}, f32[128,1024]{1,0:T(8,128)S(1)}, u32[]{:S(2)}, u32[]{:S(2)}) collective-permute-start(f32[128,1024]{1,0:T(8,128)S(1)} %collective-permute-done.7.own), channel_id=1, source_target_pairs={{0,4},{1,5},{2,6},{3,7},{4,8},{5,9},{6,10},{7,11},{8,12},{9,13},{1... | collective-permute-start | bytes 1572872 | tf_op jit(solution)/shard_map/ppermute | solution.py:27
  74.0 2.4 %collective-permute-start.18 = (f32[320,128]{1,0:T(8,128)S(1)}, f32[320,128]{1,0:T(8,128)S(1)}, u32[]{:S(2)}, u32[]{:S(2)}) collective-permute-start(f32[320,128]{1,0:T(8,128)S(1)} %add_select_fusion.3), channel_id=1, source_target_pairs={{0,48},{1,49},{2,50},{3,51},{64,112},{65,113},{66,114},{67,115},{1... | collective-permute-start | bytes 491528 | tf_op jit(solution)/shard_map/ppermute | solution.py:27
  74.7 1.7 %collective-permute-start.17 = (f32[320,128]{1,0:T(8,128)S(1)}, f32[320,128]{1,0:T(8,128)S(1)}, u32[]{:S(2)}, u32[]{:S(2)}) collective-permute-start(f32[320,128]{1,0:T(8,128)S(1)} %add_select_fusion.3), channel_id=1, source_target_pairs={{0,24},{1,25},{2,26},{3,27},{64,88},{65,89},{66,90},{67,91},{128,1... | collective-permute-start | bytes 491528 | tf_op jit(solution)/shard_map/ppermute | solution.py:27
  75.4 6.8 %collective-permute-start.20 = (f32[256,256]{1,0:T(8,128)S(1)}, f32[256,256]{1,0:T(8,128)S(1)}, u32[]{:S(2)}, u32[]{:S(2)}) collective-permute-start(f32[256,256]{1,0:T(8,128)S(1)} %copy-done.15), channel_id=1, source_target_pairs={{0,1},{1,2},{2,3},{3,0},{4,5},{5,6},{6,7},{7,4},{8,9},{9,10},{10,1... | collective-permute-start | bytes 786440 | tf_op jit(solution)/shard_map/ppermute | solution.py:27
  82.2 32.7 %copy-start.5 = (f32[128,1024]{1,0:T(8,128)}, f32[128,1024]{1,0:T(8,128)S(1)}, u32[]{:S(2)}) copy-start(f32[128,1024]{1,0:T(8,128)S(1)} %collective-permute-done.19.prev0) | copy-start | bytes 1572868
  82.2 2.4 %collective-permute-start.22 = (f32[320,128]{1,0:T(8,128)S(1)}, f32[320,128]{1,0:T(8,128)S(1)}, u32[]{:S(2)}, u32[]{:S(2)}) collective-permute-start(f32[320,128]{1,0:T(8,128)S(1)} %add_select_fusion.2), channel_id=1, source_target_pairs={{24,16},{25,17},{26,18},{27,19},{48,40},{49,41},{50,42},{51,43},{8... | collective-permute-start | bytes 491528 | tf_op jit(solution)/shard_map/ppermute | solution.py:27
  82.8 1.7 %collective-permute-start.21 = (f32[320,128]{1,0:T(8,128)S(1)}, f32[320,128]{1,0:T(8,128)S(1)}, u32[]{:S(2)}, u32[]{:S(2)}) collective-permute-start(f32[320,128]{1,0:T(8,128)S(1)} %add_select_fusion.2), channel_id=1, source_target_pairs={{0,8},{1,9},{2,10},{3,11},{24,32},{25,33},{26,34},{27,35},{48,56},... | collective-permute-start | bytes 491528 | tf_op jit(solution)/shard_map/ppermute | solution.py:27
  83.5 5.7 %collective-permute-start.23 = (f32[256,256]{1,0:T(8,128)S(1)}, f32[256,256]{1,0:T(8,128)S(1)}, u32[]{:S(2)}, u32[]{:S(2)}) collective-permute-start(f32[256,256]{1,0:T(8,128)S(1)} %collective-permute-done.20), channel_id=1, source_target_pairs={{0,64},{1,65},{2,66},{3,67},{4,68},{5,69},{6,70},{7,71},{8,72},{9,... | collective-permute-start | bytes 786440 | tf_op jit(solution)/shard_map/ppermute | solution.py:27
  89.2 25.7 %copy-start.9 = (f32[256,256]{1,0:T(8,128)}, f32[256,256]{1,0:T(8,128)S(1)}, u32[]{:S(2)}) copy-start(f32[256,256]{1,0:T(8,128)S(1)} %collective-permute-done.23.edge0) | copy-start | bytes 786436
  89.2 9.9 %collective-permute-start.24 = (f32[320,128]{1,0:T(8,128)S(1)}, f32[320,128]{1,0:T(8,128)S(1)}, u32[]{:S(2)}, u32[]{:S(2)}) collective-permute-start(f32[320,128]{1,0:T(8,128)S(1)} %add_select_fusion.1), channel_id=1, source_target_pairs={{0,4},{1,5},{2,6},{3,7},{8,12},{9,13},{10,14},{11,15},{16,20},{17,... | collective-permute-start | bytes 491528 | tf_op jit(solution)/shard_map/ppermute | solution.py:27
  90.5 16.8 %collective-permute-start.28 = (f32[256,256]{1,0:T(8,128)S(1)}, f32[256,256]{1,0:T(8,128)S(1)}, u32[]{:S(2)}, u32[]{:S(2)}) collective-permute-start(f32[256,256]{1,0:T(8,128)S(1)} %collective-permute-done.23.edge0), channel_id=1, source_target_pairs={{0,4},{1,5},{2,6},{3,7},{4,8},{5,9},{6,10},{7,11},{8,12},{9,13},{1... | collective-permute-start | bytes 786440 | tf_op jit(solution)/shard_map/ppermute | solution.py:27
  99.1 15.8 %copy-start.2 = (f32[320,128]{1,0:T(8,128)}, f32[320,128]{1,0:T(8,128)S(1)}, u32[]{:S(2)}) copy-start(f32[320,128]{1,0:T(8,128)S(1)} %broadcast_select_fusion.l0) | copy-start | bytes 491524
  99.1 9.4 %collective-permute-start.27 = (f32[320,128]{1,0:T(8,128)S(1)}, f32[320,128]{1,0:T(8,128)S(1)}, u32[]{:S(2)}, u32[]{:S(2)}) collective-permute-start(f32[320,128]{1,0:T(8,128)S(1)} %broadcast_select_fusion.l0), channel_id=1, source_target_pairs={{0,3},{1,0},{2,1},{3,2},{4,7},{5,4},{6,5},{7,6},{8,11},{9,8},{10,9... | collective-permute-start | bytes 491528 | tf_op jit(solution)/shard_map/ppermute | solution.py:27
  101.3 7.7 %collective-permute-start.26 = (f32[320,128]{1,0:T(8,128)S(1)}, f32[320,128]{1,0:T(8,128)S(1)}, u32[]{:S(2)}, u32[]{:S(2)}) collective-permute-start(f32[320,128]{1,0:T(8,128)S(1)} %broadcast_select_fusion.l0), channel_id=1, source_target_pairs={{0,2},{1,3},{2,0},{3,1},{4,6},{5,7},{6,4},{7,5},{8,10},{9,11},{10,... | collective-permute-start | bytes 491528 | tf_op jit(solution)/shard_map/ppermute | solution.py:27
  101.3 10.9 %collective-permute-start.25 = (f32[320,128]{1,0:T(8,128)S(1)}, f32[320,128]{1,0:T(8,128)S(1)}, u32[]{:S(2)}, u32[]{:S(2)}) collective-permute-start(f32[320,128]{1,0:T(8,128)S(1)} %broadcast_select_fusion.l0), channel_id=1, source_target_pairs={{0,1},{1,2},{2,3},{3,0},{4,5},{5,6},{6,7},{7,4},{8,9},{9,10},{10,1... | collective-permute-start | bytes 491528 | tf_op jit(solution)/shard_map/ppermute | solution.py:27
  107.4 7.6 %copy-start.10 = (f32[256,256]{1,0:T(8,128)}, f32[256,256]{1,0:T(8,128)S(1)}, u32[]{:S(2)}) copy-start(f32[256,256]{1,0:T(8,128)S(1)} %collective-permute-done.28.edge1) | copy-start | bytes 786436
  108.5 6.4 %copy-start.12 = (f32[320,128]{1,0:T(8,128)}, f32[320,128]{1,0:T(8,128)S(1)}, u32[]{:S(2)}) copy-start(f32[320,128]{1,0:T(8,128)S(1)} %collective-permute-done.27.l3) | copy-start | bytes 491524
  109.0 6.0 %copy-start.13 = (f32[320,128]{1,0:T(8,128)}, f32[320,128]{1,0:T(8,128)S(1)}, u32[]{:S(2)}) copy-start(f32[320,128]{1,0:T(8,128)S(1)} %collective-permute-done.26.l2) | copy-start | bytes 491524
  112.2 2.7 %copy-start.14 = (f32[320,128]{1,0:T(8,128)}, f32[320,128]{1,0:T(8,128)S(1)}, u32[]{:S(2)}) copy-start(f32[320,128]{1,0:T(8,128)S(1)} %collective-permute-done.25.l1) | copy-start | bytes 491524
Sparse Core Ops, SparseCore 0:
  69.7 45.1 all-gather.1

commit v4 on v3

--- a/solution.py
+++ b/solution.py
@@ -121,7 +121,6 @@
 
 def reciprocal(d):
     r = pl.reciprocal(d, approx=True)
-    r = r * (2.0 - d * r)
     return r * (2.0 - d * r)
 
 

time: 134 us -> 134 us (level)
  no operation moved by 1% of the time
where the time goes in v4:
time: 134 us
  starting transfers between devices  44.7 us (33%)
  Pallas kernels  39.1 us (29%)
  waiting for transfers between devices  32.5 us (24%)
  between operations  15.1 us (11%)
  local copies, waits for them, and re-layouts  2.05 us (2%)
    ppermute x29, starting transfers between devices, permute(): return lax.ppermute(x, AXES, pairs)  44.7 us
    ppermute x29, waiting for transfers between devices, permute(): return lax.ppermute(x, AXES, pairs)  29.3 us
    pallas_call x1, Pallas kernels, first_call(): pl.pallas_call(first_kernel, grid=(1,), in_specs=[whole((128, 512))] * 4,...  12 us
    pallas_call x1, Pallas kernels, second_call(): pl.pallas_call(second_kernel, grid=(1,), in_specs=[whole(HALF)] * 3, out_...  12 us
    pallas_call x1, Pallas kernels, update_call(): pl.pallas_call(update_kernel, grid=(1,), in_specs=[smem(), smem()] + [who...  11.7 us
    all_gather x1, waiting for transfers between devices, body(): a_col = lax.all_gather(piece, 'row', axis=0, tiled=True)  3.18 us
  transfers between devices with their start and end apart: 30, of which 10 were waited for; matrix products, arithmetic and copies ran while one was open for 1% of the time, Pallas kernels for 18%

profile of v4, /device:TPU:1, one launch (start us, length us, event | category | flops | bytes accessed | tf_op | source)
XLA Modules:
  0.0 133.7 jit_solution(1535738719577074101)
XLA Ops:
  7.2 0.0 copy-start
  7.2 0.0 all-gather.2.cloned.1.call-start
  7.2 2.6 %pack.1 = (f32[128,128]{1,0:T(8,128)}, f32[256,128]{1,0:T(8,128)}, f32[128,256]{1,0:T(8,128)}, f32[256,256]{1,0:T(8,128)}, f32[128,1024]{1,0:T(8,128)}, /*index=5*/f32[128,1024]{1,0:T(8,128)}) custom-call(f32[256,1024]{1,0:T(8,128)} %bitcast.4, f32[256,1024]{1,0:T(8,128)} %bitcast.5, f32[256,1024]{1,0:T(8,128)} %bitcast.6), custom_call_target="tpu_custom_call" | custom-call | tf_op jit(solution)/shard_map/pack/pallas_call | solution.py:72
  9.8 1.3 collective-permute-start.3
  11.1 5.9 %collective-permute-start.1 = (f32[256,128]{1,0:T(8,128)}, f32[256,128]{1,0:T(8,128)S(1)}, u32[]{:S(2)}, u32[]{:S(2)}) collective-permute-start(f32[256,128]{1,0:T(8,128)} %get-tuple-element.48), channel_id=1, source_target_pairs={{0,68},{4,72},{8,76},{12,80},{16,84},{20,88},{24,92},{28,96},{32,1... | collective-permute-start | bytes 393224 | tf_op jit(solution)/shard_map/ppermute | solution.py:27
  16.9 1.3 collective-permute-start.2
  18.2 2.2 %collective-permute-start = (f32[128,128]{1,0:T(8,128)}, f32[128,128]{1,0:T(8,128)S(1)}, u32[]{:S(2)}, u32[]{:S(2)}) collective-permute-start(f32[128,128]{1,0:T(8,128)} %get-tuple-element.47), channel_id=1, source_target_pairs={{0,64},{4,68},{8,72},{12,76},{16,80},{20,84},{24,88},{28,92},{32,9... | collective-permute-start | bytes 196616 | tf_op jit(solution)/shard_map/ppermute | solution.py:27
  21.1 1.3 slice.4.front
  22.4 2.2 %collective-permute-done.ea = f32[128,128]{1,0:T(8,128)S(1)} collective-permute-done((f32[128,128]{1,0:T(8,128)}, f32[128,128]{1,0:T(8,128)S(1)}, u32[]{:S(2)}, u32[]{:S(2)}) %collective-permute-start) | collective-permute-done | bytes 65568 | tf_op jit(solution)/shard_map/ppermute | solution.py:27
  24.6 0.0 collective-permute-done.1.eb
  24.6 3.3 %collective-permute-done.2.ed = f32[128,256]{1,0:T(8,128)S(1)} collective-permute-done((f32[128,256]{1,0:T(8,128)}, f32[128,256]{1,0:T(8,128)S(1)}, u32[]{:S(2)}, u32[]{:S(2)}) %collective-permute-start.2) | collective-permute-done | bytes 131104 | tf_op jit(solution)/shard_map/ppermute | solution.py:27
  27.9 0.0 collective-permute-done.3.ee
  27.9 0.9 panel.1
  28.8 1.3 collective-permute-start.4
  30.1 1.3 collective-permute-start.5
  31.4 1.3 collective-permute-start.6
  32.7 0.3 collective-permute-start.7
  33.0 1.9 %collective-permute-start.8 = (f32[128,1024]{1,0:T(8,128)}, f32[128,1024]{1,0:T(8,128)S(1)}, u32[]{:S(2)}, u32[]{:S(2)}) collective-permute-start(f32[128,1024]{1,0:T(8,128)} %get-tuple-element.58), channel_id=1, source_target_pairs={{0,4},{1,5},{2,6},{3,7},{4,8},{5,9},{6,10},{7,11},{8,12},{9,13},{1... | collective-permute-start | bytes 1572872 | tf_op jit(solution)/shard_map/ppermute | solution.py:27
  34.8 12.0 %first.1 = (f32[256,256]{1,0:T(8,128)S(1)}, f32[256,256]{1,0:T(8,128)S(1)}, f32[256,256]{1,0:T(8,128)S(1)}) custom-call(f32[128,512]{1,0:T(8,128)S(1)} %get-tuple-element.51.q0, f32[128,512]{1,0:T(8,128)S(1)} %get-tuple-element.52.q1, f32[128,512]{1,0:T(8,128)S(1)} %get-tuple-element.53.q2, f32[128,512]{1,0:T(8,128)S(1)} %get-tuple-element.54.q3), custom_call_target="tpu_custom_call" | custom-call | flops 10000000000 | bytes 4194304 | tf_op jit(solution)/shard_map/first/pallas_call | solution.py:220
  46.8 0.0 collective-permute-done.5
  46.9 0.0 collective-permute-done.6
  46.9 0.0 collective-permute-done.8
  46.9 0.1 add_select_fusion.a0
  47.0 0.1 collective-permute-start.13
  47.1 0.1 collective-permute-start.12
  47.2 1.4 %collective-permute-start.11 = (f32[128,512]{1,0:T(8,128)S(1)}, f32[128,512]{1,0:T(8,128)S(1)}, u32[]{:S(2)}, u32[]{:S(2)}) collective-permute-start(f32[128,512]{1,0:T(8,128)S(1)} %add_select_fusion.a0), channel_id=1, source_target_pairs={{0,1},{1,2},{2,3},{3,0},{4,5},{5,6},{6,7},{7,4},{8,9},{9,10},{10,1... | collective-permute-start | bytes 786440 | tf_op jit(solution)/shard_map/ppermute | solution.py:27
  48.6 4.2 %collective-permute-start.9 = (f32[128,512]{1,0:T(8,128)S(1)}, f32[128,512]{1,0:T(8,128)S(1)}, u32[]{:S(2)}, u32[]{:S(2)}) collective-permute-start(f32[128,512]{1,0:T(8,128)S(1)} %add_select_fusion.a0), channel_id=1, source_target_pairs={{0,0},{1,4},{2,8},{3,12},{4,16},{5,20},{6,24},{7,28},{8,32},{9,36}... | collective-permute-start | bytes 786440 | tf_op jit(solution)/shard_map/ppermute | solution.py:27
  52.8 1.0 collective-permute-start.10
  53.7 12.0 %second.1 = (f32[320,128]{1,0:T(8,128)S(1)}, f32[320,128]{1,0:T(8,128)S(1)}, f32[320,128]{1,0:T(8,128)S(1)}, f32[320,128]{1,0:T(8,128)S(1)}) custom-call(f32[256,256]{1,0:T(8,128)S(1)} %get-tuple-element.67.inv, f32[256,256]{1,0:T(8,128)S(1)} %get-tuple-element.68.below, f32[256,256]{1,0:T(8,128)S(1)} %get-tuple-element.69.rest), custom_call_target="tpu_custom_call" | custom-call | flops 10000000000 | bytes 4194304 | tf_op jit(solution)/shard_map/second/pallas_call | solution.py:260
  65.7 0.0 collective-permute-done.13.a3
  65.7 0.0 collective-permute-done.12.a2
  65.8 2.6 %collective-permute-done.9 = f32[128,512]{1,0:T(8,128)S(1)} collective-permute-done((f32[128,512]{1,0:T(8,128)S(1)}, f32[128,512]{1,0:T(8,128)S(1)}, u32[]{:S(2)}, u32[]{:S(2)}) %collective-permute-start.9) | collective-permute-done | bytes 262176 | tf_op jit(solution)/shard_map/ppermute | solution.py:27
  68.4 0.0 collective-permute-done.10.prev1
  68.4 0.7 copy-done.11
  69.1 0.0 all-gather.2.cloned.1.call-update
  69.1 0.7 collective-permute-start.14
  69.8 0.7 collective-permute-start.15
  70.5 0.7 collective-permute-start.16
  71.2 2.4 %collective-permute-start.19 = (f32[128,1024]{1,0:T(8,128)S(1)}, f32[128,1024]{1,0:T(8,128)S(1)}, u32[]{:S(2)}, u32[]{:S(2)}) collective-permute-start(f32[128,1024]{1,0:T(8,128)S(1)} %collective-permute-done.7.own), channel_id=1, source_target_pairs={{0,4},{1,5},{2,6},{3,7},{4,8},{5,9},{6,10},{7,11},{8,12},{9,13},{1... | collective-permute-start | bytes 1572872 | tf_op jit(solution)/shard_map/ppermute | solution.py:27
  73.6 0.0 collective-permute-done.14
  73.6 0.0 collective-permute-done.15
  73.6 0.0 collective-permute-done.16
  73.6 0.7 collective-permute-start.18
  74.3 0.7 collective-permute-start.17
  75.0 1.0 collective-permute-start.20
  76.1 5.7 %collective-permute-done.20 = f32[256,256]{1,0:T(8,128)S(1)} collective-permute-done((f32[256,256]{1,0:T(8,128)S(1)}, f32[256,256]{1,0:T(8,128)S(1)}, u32[]{:S(2)}, u32[]{:S(2)}) %collective-permute-start.20) | collective-permute-done | bytes 262176 | tf_op jit(solution)/shard_map/ppermute | solution.py:27
  81.8 0.0 collective-permute-done.19.prev0
  81.8 0.7 collective-permute-start.22
  82.5 0.7 collective-permute-start.21
  83.2 0.6 collective-permute-start.23
  83.8 0.0 collective-permute-done.22
  83.8 0.0 collective-permute-done.21
  83.9 5.0 %collective-permute-done.23.edge0 = f32[256,256]{1,0:T(8,128)S(1)} collective-permute-done((f32[256,256]{1,0:T(8,128)S(1)}, f32[256,256]{1,0:T(8,128)S(1)}, u32[]{:S(2)}, u32[]{:S(2)}) %collective-permute-start.23) | collective-permute-done | bytes 262176 | tf_op jit(solution)/shard_map/ppermute | solution.py:27
  88.9 1.3 collective-permute-start.24
  90.2 8.8 %collective-permute-start.28 = (f32[256,256]{1,0:T(8,128)S(1)}, f32[256,256]{1,0:T(8,128)S(1)}, u32[]{:S(2)}, u32[]{:S(2)}) collective-permute-start(f32[256,256]{1,0:T(8,128)S(1)} %collective-permute-done.23.edge0), channel_id=1, source_target_pairs={{0,4},{1,5},{2,6},{3,7},{4,8},{5,9},{6,10},{7,11},{8,12},{9,13},{1... | collective-permute-start | bytes 786440 | tf_op jit(solution)/shard_map/ppermute | solution.py:27
  99.0 0.0 collective-permute-done.24
  99.0 1.8 %collective-permute-start.27 = (f32[320,128]{1,0:T(8,128)S(1)}, f32[320,128]{1,0:T(8,128)S(1)}, u32[]{:S(2)}, u32[]{:S(2)}) collective-permute-start(f32[320,128]{1,0:T(8,128)S(1)} %broadcast_select_fusion.l0), channel_id=1, source_target_pairs={{0,3},{1,0},{2,1},{3,2},{4,7},{5,4},{6,5},{7,6},{8,11},{9,8},{10,9... | collective-permute-start | bytes 491528 | tf_op jit(solution)/shard_map/ppermute | solution.py:27
  100.8 0.7 collective-permute-start.25
  101.5 6.1 %collective-permute-done.28.edge1 = f32[256,256]{1,0:T(8,128)S(1)} collective-permute-done((f32[256,256]{1,0:T(8,128)S(1)}, f32[256,256]{1,0:T(8,128)S(1)}, u32[]{:S(2)}, u32[]{:S(2)}) %collective-permute-start.28) | collective-permute-done | bytes 262176 | tf_op jit(solution)/shard_map/ppermute | solution.py:27
  107.5 0.5 collective-permute-done.27.l3
  108.1 0.5 collective-permute-done.26.l2
  108.6 3.3 %collective-permute-done.25.l1 = f32[320,128]{1,0:T(8,128)S(1)} collective-permute-done((f32[320,128]{1,0:T(8,128)S(1)}, f32[320,128]{1,0:T(8,128)S(1)}, u32[]{:S(2)}, u32[]{:S(2)}) %collective-permute-start.25) | collective-permute-done | bytes 163872 | tf_op jit(solution)/shard_map/ppermute | solution.py:27
  111.8 3.2 %all-gather.2.cloned.1.call-done.a_col = f32[2048,512]{1,0:T(8,128)} async-done(((f32[128,512]{1,0:T(8,128)}), f32[2048,512]{1,0:T(8,128)}) %all-gather.2.cloned.1.call-update) | async-done | bytes 4194320 | tf_op jit(solution)/shard_map/all_gather | solution.py:455
  115.1 11.7 %update.1 = (f32[512,512]{1,0:T(8,128)}, f32[512,2048]{1,0:T(8,128)}) custom-call(s32[1,32]{1,0:T(1,128)} %bmap.3, s32[1]{0:T(128)S(6)} %copy.6.order, f32[320,128]{1,0:T(8,128)} %copy-done.2, f32[320,128]{1,0:T(8,128)} %copy-done.14, f32[320,128]{1,0:T(8,128)} %copy-done.13, f32[320,128]{1,0:T(8,128)} %copy-done.12, f32[128,512]{1,0:T(8,128)} %copy-done.1, ...), custom_call_target="tpu_custom_call" | custom-call | tf_op jit(solution)/shard_map/update/pallas_call | solution.py:377
  (40 shorter events, 0.2 us)
Async XLA Ops:
  7.2 20.7 %copy-start = (s32[1,32]{1,0:T(1,128)S(1)}, s32[1,32]{1,0:T(1,128)}, u32[]{:S(2)}) copy-start(s32[1,32]{1,0:T(1,128)} %bmap.3) | copy-start | bytes 388
  7.2 107.8 %all-gather.2.cloned.1.call-start = ((), (), s32[]{:S(2)}) async-start(), calls=%async_computation | async-start | bytes 4456448 | tf_op jit(solution)/shard_map/all_gather | solution.py:455
  9.8 18.1 %collective-permute-start.3 = (f32[256,256]{1,0:T(8,128)}, f32[256,256]{1,0:T(8,128)S(1)}, u32[]{:S(2)}, u32[]{:S(2)}) collective-permute-start(f32[256,256]{1,0:T(8,128)} %get-tuple-element.79), channel_id=1, source_target_pairs={{3,68},{7,72},{11,76},{15,80},{19,84},{23,88},{27,92},{31,96},{35,... | collective-permute-start | bytes 786440 | tf_op jit(solution)/shard_map/ppermute | solution.py:27
  11.1 13.5 %collective-permute-start.1 = (f32[256,128]{1,0:T(8,128)}, f32[256,128]{1,0:T(8,128)S(1)}, u32[]{:S(2)}, u32[]{:S(2)}) collective-permute-start(f32[256,128]{1,0:T(8,128)} %get-tuple-element.48), channel_id=1, source_target_pairs={{0,68},{4,72},{8,76},{12,80},{16,84},{20,88},{24,92},{28,96},{32,1... | collective-permute-start | bytes 393224 | tf_op jit(solution)/shard_map/ppermute | solution.py:27
  16.9 10.9 %collective-permute-start.2 = (f32[128,256]{1,0:T(8,128)}, f32[128,256]{1,0:T(8,128)S(1)}, u32[]{:S(2)}, u32[]{:S(2)}) collective-permute-start(f32[128,256]{1,0:T(8,128)} %get-tuple-element.49), channel_id=1, source_target_pairs={{3,64},{7,68},{11,72},{15,76},{19,80},{23,84},{27,88},{31,92},{35,... | collective-permute-start | bytes 393224 | tf_op jit(solution)/shard_map/ppermute | solution.py:27
  18.2 6.3 %collective-permute-start = (f32[128,128]{1,0:T(8,128)}, f32[128,128]{1,0:T(8,128)S(1)}, u32[]{:S(2)}, u32[]{:S(2)}) collective-permute-start(f32[128,128]{1,0:T(8,128)} %get-tuple-element.47), channel_id=1, source_target_pairs={{0,64},{4,68},{8,72},{12,76},{16,80},{20,84},{24,88},{28,92},{32,9... | collective-permute-start | bytes 196616 | tf_op jit(solution)/shard_map/ppermute | solution.py:27
  28.8 18.1 %collective-permute-start.4 = (f32[128,512]{1,0:T(8,128)S(1)}, f32[128,512]{1,0:T(8,128)S(1)}, u32[]{:S(2)}, u32[]{:S(2)}) collective-permute-start(f32[128,512]{1,0:T(8,128)S(1)} %get-tuple-element.52.q1), channel_id=1, source_target_pairs={{0,1},{4,5},{8,9},{12,13},{16,17},{20,21},{24,25},{28,29},{32,33},... | collective-permute-start | bytes 786440 | tf_op jit(solution)/shard_map/ppermute | solution.py:27
  30.1 16.8 %collective-permute-start.5 = (f32[128,512]{1,0:T(8,128)S(1)}, f32[128,512]{1,0:T(8,128)S(1)}, u32[]{:S(2)}, u32[]{:S(2)}) collective-permute-start(f32[128,512]{1,0:T(8,128)S(1)} %get-tuple-element.53.q2), channel_id=1, source_target_pairs={{0,2},{4,6},{8,10},{12,14},{16,18},{20,22},{24,26},{28,30},{32,34}... | collective-permute-start | bytes 786440 | tf_op jit(solution)/shard_map/ppermute | solution.py:27
  31.4 15.5 %collective-permute-start.6 = (f32[128,512]{1,0:T(8,128)S(1)}, f32[128,512]{1,0:T(8,128)S(1)}, u32[]{:S(2)}, u32[]{:S(2)}) collective-permute-start(f32[128,512]{1,0:T(8,128)S(1)} %get-tuple-element.54.q3), channel_id=1, source_target_pairs={{0,3},{4,7},{8,11},{12,15},{16,19},{20,23},{24,27},{28,31},{32,35}... | collective-permute-start | bytes 786440 | tf_op jit(solution)/shard_map/ppermute | solution.py:27
  32.7 14.2 %collective-permute-start.7 = (f32[128,1024]{1,0:T(8,128)}, f32[128,1024]{1,0:T(8,128)S(1)}, u32[]{:S(2)}, u32[]{:S(2)}) collective-permute-start(f32[128,1024]{1,0:T(8,128)} %get-tuple-element.57), channel_id=1, source_target_pairs={{0,64},{1,65},{2,66},{3,67},{4,68},{5,69},{6,70},{7,71},{8,72},{9,... | collective-permute-start | bytes 1572872 | tf_op jit(solution)/shard_map/ppermute | solution.py:27
  33.0 13.9 %collective-permute-start.8 = (f32[128,1024]{1,0:T(8,128)}, f32[128,1024]{1,0:T(8,128)S(1)}, u32[]{:S(2)}, u32[]{:S(2)}) collective-permute-start(f32[128,1024]{1,0:T(8,128)} %get-tuple-element.58), channel_id=1, source_target_pairs={{0,4},{1,5},{2,6},{3,7},{4,8},{5,9},{6,10},{7,11},{8,12},{9,13},{1... | collective-permute-start | bytes 1572872 | tf_op jit(solution)/shard_map/ppermute | solution.py:27
  46.9 24.3 %copy-start.3 = (f32[128,1024]{1,0:T(8,128)}, f32[128,1024]{1,0:T(8,128)S(1)}, u32[]{:S(2)}) copy-start(f32[128,1024]{1,0:T(8,128)S(1)} %collective-permute-done.7.own) | copy-start | bytes 1572868
  47.0 18.7 %copy-start.1 = (f32[128,512]{1,0:T(8,128)}, f32[128,512]{1,0:T(8,128)S(1)}, u32[]{:S(2)}) copy-start(f32[128,512]{1,0:T(8,128)S(1)} %add_select_fusion.a0) | copy-start | bytes 786436
  47.0 18.7 %collective-permute-start.13 = (f32[128,512]{1,0:T(8,128)S(1)}, f32[128,512]{1,0:T(8,128)S(1)}, u32[]{:S(2)}, u32[]{:S(2)}) collective-permute-start(f32[128,512]{1,0:T(8,128)S(1)} %add_select_fusion.a0), channel_id=1, source_target_pairs={{0,3},{1,0},{2,1},{3,2},{4,7},{5,4},{6,5},{7,6},{8,11},{9,8},{10,9... | collective-permute-start | bytes 786440 | tf_op jit(solution)/shard_map/ppermute | solution.py:27
  47.1 18.6 %collective-permute-start.12 = (f32[128,512]{1,0:T(8,128)S(1)}, f32[128,512]{1,0:T(8,128)S(1)}, u32[]{:S(2)}, u32[]{:S(2)}) collective-permute-start(f32[128,512]{1,0:T(8,128)S(1)} %add_select_fusion.a0), channel_id=1, source_target_pairs={{0,2},{1,3},{2,0},{3,1},{4,6},{5,7},{6,4},{7,5},{8,10},{9,11},{10,... | collective-permute-start | bytes 786440 | tf_op jit(solution)/shard_map/ppermute | solution.py:27
  47.2 18.5 %collective-permute-start.11 = (f32[128,512]{1,0:T(8,128)S(1)}, f32[128,512]{1,0:T(8,128)S(1)}, u32[]{:S(2)}, u32[]{:S(2)}) collective-permute-start(f32[128,512]{1,0:T(8,128)S(1)} %add_select_fusion.a0), channel_id=1, source_target_pairs={{0,1},{1,2},{2,3},{3,0},{4,5},{5,6},{6,7},{7,4},{8,9},{9,10},{10,1... | collective-permute-start | bytes 786440 | tf_op jit(solution)/shard_map/ppermute | solution.py:27
  48.6 19.8 %collective-permute-start.9 = (f32[128,512]{1,0:T(8,128)S(1)}, f32[128,512]{1,0:T(8,128)S(1)}, u32[]{:S(2)}, u32[]{:S(2)}) collective-permute-start(f32[128,512]{1,0:T(8,128)S(1)} %add_select_fusion.a0), channel_id=1, source_target_pairs={{0,0},{1,4},{2,8},{3,12},{4,16},{5,20},{6,24},{7,28},{8,32},{9,36}... | collective-permute-start | bytes 786440 | tf_op jit(solution)/shard_map/ppermute | solution.py:27
  52.8 22.2 %copy-start.15 = (f32[256,256]{1,0:T(8,128)S(1)}, f32[256,256]{1,0:T(8,128)}, u32[]{:S(2)}) copy-start(f32[256,256]{1,0:T(8,128)} %get-tuple-element.79) | copy-start | bytes 786436
  52.8 15.6 %collective-permute-start.10 = (f32[128,1024]{1,0:T(8,128)S(1)}, f32[128,1024]{1,0:T(8,128)S(1)}, u32[]{:S(2)}, u32[]{:S(2)}) collective-permute-start(f32[128,1024]{1,0:T(8,128)S(1)} %collective-permute-done.8), channel_id=1, source_target_pairs={{0,64},{1,65},{2,66},{3,67},{4,68},{5,69},{6,70},{7,71},{8,72},{9,... | collective-permute-start | bytes 1572872 | tf_op jit(solution)/shard_map/ppermute | solution.py:27
  65.7 49.3 %copy-start.6 = (f32[128,512]{1,0:T(8,128)}, f32[128,512]{1,0:T(8,128)S(1)}, u32[]{:S(2)}) copy-start(f32[128,512]{1,0:T(8,128)S(1)} %collective-permute-done.13.a3) | copy-start | bytes 786436
  65.7 49.3 %copy-start.7 = (f32[128,512]{1,0:T(8,128)}, f32[128,512]{1,0:T(8,128)S(1)}, u32[]{:S(2)}) copy-start(f32[128,512]{1,0:T(8,128)S(1)} %collective-permute-done.12.a2) | copy-start | bytes 786436
  65.8 49.3 %copy-start.8 = (f32[128,512]{1,0:T(8,128)}, f32[128,512]{1,0:T(8,128)S(1)}, u32[]{:S(2)}) copy-start(f32[128,512]{1,0:T(8,128)S(1)} %collective-permute-done.11.a1) | copy-start | bytes 786436
  68.4 0.7 copy-start.11
  68.4 46.6 %copy-start.4 = (f32[128,1024]{1,0:T(8,128)}, f32[128,1024]{1,0:T(8,128)S(1)}, u32[]{:S(2)}) copy-start(f32[128,1024]{1,0:T(8,128)S(1)} %collective-permute-done.10.prev1) | copy-start | bytes 1572868
  69.1 4.5 %collective-permute-start.14 = (f32[320,128]{1,0:T(8,128)S(1)}, f32[320,128]{1,0:T(8,128)S(1)}, u32[]{:S(2)}, u32[]{:S(2)}) collective-permute-start(f32[320,128]{1,0:T(8,128)S(1)} %get-tuple-element.75), channel_id=1, source_target_pairs={{0,1},{64,65},{128,129},{192,193}} | collective-permute-start | bytes 491528 | tf_op jit(solution)/shard_map/ppermute | solution.py:27
  69.8 3.8 %collective-permute-start.15 = (f32[320,128]{1,0:T(8,128)S(1)}, f32[320,128]{1,0:T(8,128)S(1)}, u32[]{:S(2)}, u32[]{:S(2)}) collective-permute-start(f32[320,128]{1,0:T(8,128)S(1)} %get-tuple-element.76), channel_id=1, source_target_pairs={{0,2},{64,66},{128,130},{192,194}} | collective-permute-start | bytes 491528 | tf_op jit(solution)/shard_map/ppermute | solution.py:27
  70.5 3.1 %collective-permute-start.16 = (f32[320,128]{1,0:T(8,128)S(1)}, f32[320,128]{1,0:T(8,128)S(1)}, u32[]{:S(2)}, u32[]{:S(2)}) collective-permute-start(f32[320,128]{1,0:T(8,128)S(1)} %get-tuple-element.77), channel_id=1, source_target_pairs={{0,3},{64,67},{128,131},{192,195}} | collective-permute-start | bytes 491528 | tf_op jit(solution)/shard_map/ppermute | solution.py:27
  71.2 10.7 %collective-permute-start.19 = (f32[128,1024]{1,0:T(8,128)S(1)}, f32[128,1024]{1,0:T(8,128)S(1)}, u32[]{:S(2)}, u32[]{:S(2)}) collective-permute-start(f32[128,1024]{1,0:T(8,128)S(1)} %collective-permute-done.7.own), channel_id=1, source_target_pairs={{0,4},{1,5},{2,6},{3,7},{4,8},{5,9},{6,10},{7,11},{8,12},{9,13},{1... | collective-permute-start | bytes 1572872 | tf_op jit(solution)/shard_map/ppermute | solution.py:27
  73.6 2.4 %collective-permute-start.18 = (f32[320,128]{1,0:T(8,128)S(1)}, f32[320,128]{1,0:T(8,128)S(1)}, u32[]{:S(2)}, u32[]{:S(2)}) collective-permute-start(f32[320,128]{1,0:T(8,128)S(1)} %add_select_fusion.3), channel_id=1, source_target_pairs={{0,48},{1,49},{2,50},{3,51},{64,112},{65,113},{66,114},{67,115},{1... | collective-permute-start | bytes 491528 | tf_op jit(solution)/shard_map/ppermute | solution.py:27
  74.3 1.7 %collective-permute-start.17 = (f32[320,128]{1,0:T(8,128)S(1)}, f32[320,128]{1,0:T(8,128)S(1)}, u32[]{:S(2)}, u32[]{:S(2)}) collective-permute-start(f32[320,128]{1,0:T(8,128)S(1)} %add_select_fusion.3), channel_id=1, source_target_pairs={{0,24},{1,25},{2,26},{3,27},{64,88},{65,89},{66,90},{67,91},{128,1... | collective-permute-start | bytes 491528 | tf_op jit(solution)/shard_map/ppermute | solution.py:27
  75.0 6.8 %collective-permute-start.20 = (f32[256,256]{1,0:T(8,128)S(1)}, f32[256,256]{1,0:T(8,128)S(1)}, u32[]{:S(2)}, u32[]{:S(2)}) collective-permute-start(f32[256,256]{1,0:T(8,128)S(1)} %copy-done.15), channel_id=1, source_target_pairs={{0,1},{1,2},{2,3},{3,0},{4,5},{5,6},{6,7},{7,4},{8,9},{9,10},{10,1... | collective-permute-start | bytes 786440 | tf_op jit(solution)/shard_map/ppermute | solution.py:27
  81.8 33.2 %copy-start.5 = (f32[128,1024]{1,0:T(8,128)}, f32[128,1024]{1,0:T(8,128)S(1)}, u32[]{:S(2)}) copy-start(f32[128,1024]{1,0:T(8,128)S(1)} %collective-permute-done.19.prev0) | copy-start | bytes 1572868
  81.8 2.0 %collective-permute-start.22 = (f32[320,128]{1,0:T(8,128)S(1)}, f32[320,128]{1,0:T(8,128)S(1)}, u32[]{:S(2)}, u32[]{:S(2)}) collective-permute-start(f32[320,128]{1,0:T(8,128)S(1)} %add_select_fusion.2), channel_id=1, source_target_pairs={{24,16},{25,17},{26,18},{27,19},{48,40},{49,41},{50,42},{51,43},{8... | collective-permute-start | bytes 491528 | tf_op jit(solution)/shard_map/ppermute | solution.py:27
  82.5 1.3 collective-permute-start.21
  83.2 5.7 %collective-permute-start.23 = (f32[256,256]{1,0:T(8,128)S(1)}, f32[256,256]{1,0:T(8,128)S(1)}, u32[]{:S(2)}, u32[]{:S(2)}) collective-permute-start(f32[256,256]{1,0:T(8,128)S(1)} %collective-permute-done.20), channel_id=1, source_target_pairs={{0,64},{1,65},{2,66},{3,67},{4,68},{5,69},{6,70},{7,71},{8,72},{9,... | collective-permute-start | bytes 786440 | tf_op jit(solution)/shard_map/ppermute | solution.py:27
  88.9 26.2 %copy-start.9 = (f32[256,256]{1,0:T(8,128)}, f32[256,256]{1,0:T(8,128)S(1)}, u32[]{:S(2)}) copy-start(f32[256,256]{1,0:T(8,128)S(1)} %collective-permute-done.23.edge0) | copy-start | bytes 786436
  88.9 10.1 %collective-permute-start.24 = (f32[320,128]{1,0:T(8,128)S(1)}, f32[320,128]{1,0:T(8,128)S(1)}, u32[]{:S(2)}, u32[]{:S(2)}) collective-permute-start(f32[320,128]{1,0:T(8,128)S(1)} %add_select_fusion.1), channel_id=1, source_target_pairs={{0,4},{1,5},{2,6},{3,7},{8,12},{9,13},{10,14},{11,15},{16,20},{17,... | collective-permute-start | bytes 491528 | tf_op jit(solution)/shard_map/ppermute | solution.py:27
  90.2 17.4 %collective-permute-start.28 = (f32[256,256]{1,0:T(8,128)S(1)}, f32[256,256]{1,0:T(8,128)S(1)}, u32[]{:S(2)}, u32[]{:S(2)}) collective-permute-start(f32[256,256]{1,0:T(8,128)S(1)} %collective-permute-done.23.edge0), channel_id=1, source_target_pairs={{0,4},{1,5},{2,6},{3,7},{4,8},{5,9},{6,10},{7,11},{8,12},{9,13},{1... | collective-permute-start | bytes 786440 | tf_op jit(solution)/shard_map/ppermute | solution.py:27
  99.0 16.1 %copy-start.2 = (f32[320,128]{1,0:T(8,128)}, f32[320,128]{1,0:T(8,128)S(1)}, u32[]{:S(2)}) copy-start(f32[320,128]{1,0:T(8,128)S(1)} %broadcast_select_fusion.l0) | copy-start | bytes 491524
  99.0 9.1 %collective-permute-start.27 = (f32[320,128]{1,0:T(8,128)S(1)}, f32[320,128]{1,0:T(8,128)S(1)}, u32[]{:S(2)}, u32[]{:S(2)}) collective-permute-start(f32[320,128]{1,0:T(8,128)S(1)} %broadcast_select_fusion.l0), channel_id=1, source_target_pairs={{0,3},{1,0},{2,1},{3,2},{4,7},{5,4},{6,5},{7,6},{8,11},{9,8},{10,9... | collective-permute-start | bytes 491528 | tf_op jit(solution)/shard_map/ppermute | solution.py:27
  100.8 7.8 %collective-permute-start.26 = (f32[320,128]{1,0:T(8,128)S(1)}, f32[320,128]{1,0:T(8,128)S(1)}, u32[]{:S(2)}, u32[]{:S(2)}) collective-permute-start(f32[320,128]{1,0:T(8,128)S(1)} %broadcast_select_fusion.l0), channel_id=1, source_target_pairs={{0,2},{1,3},{2,0},{3,1},{4,6},{5,7},{6,4},{7,5},{8,10},{9,11},{10,... | collective-permute-start | bytes 491528 | tf_op jit(solution)/shard_map/ppermute | solution.py:27
  100.8 11.0 %collective-permute-start.25 = (f32[320,128]{1,0:T(8,128)S(1)}, f32[320,128]{1,0:T(8,128)S(1)}, u32[]{:S(2)}, u32[]{:S(2)}) collective-permute-start(f32[320,128]{1,0:T(8,128)S(1)} %broadcast_select_fusion.l0), channel_id=1, source_target_pairs={{0,1},{1,2},{2,3},{3,0},{4,5},{5,6},{6,7},{7,4},{8,9},{9,10},{10,1... | collective-permute-start | bytes 491528 | tf_op jit(solution)/shard_map/ppermute | solution.py:27
  107.5 7.5 %copy-start.10 = (f32[256,256]{1,0:T(8,128)}, f32[256,256]{1,0:T(8,128)S(1)}, u32[]{:S(2)}) copy-start(f32[256,256]{1,0:T(8,128)S(1)} %collective-permute-done.28.edge1) | copy-start | bytes 786436
  108.1 7.0 %copy-start.12 = (f32[320,128]{1,0:T(8,128)}, f32[320,128]{1,0:T(8,128)S(1)}, u32[]{:S(2)}) copy-start(f32[320,128]{1,0:T(8,128)S(1)} %collective-permute-done.27.l3) | copy-start | bytes 491524
  108.6 6.5 %copy-start.13 = (f32[320,128]{1,0:T(8,128)}, f32[320,128]{1,0:T(8,128)S(1)}, u32[]{:S(2)}) copy-start(f32[320,128]{1,0:T(8,128)S(1)} %collective-permute-done.26.l2) | copy-start | bytes 491524
  111.8 3.3 %copy-start.14 = (f32[320,128]{1,0:T(8,128)}, f32[320,128]{1,0:T(8,128)S(1)}, u32[]{:S(2)}) copy-start(f32[320,128]{1,0:T(8,128)S(1)} %collective-permute-done.25.l1) | copy-start | bytes 491524
Sparse Core Ops, SparseCore 0:
  69.2 45.7 all-gather.1
